TPU v7x, 32 devices: a whole 2x2x4 slice. The times are simulated.
32 devices in a mesh: path: 8 (over z, y), shard: 4 (over x, core).
Axes of the slice: x: 2, y: 2, z: 4, core: 2. Of those that a mesh axis runs over, the one named last changes fastest.
Arguments:
- tokens: bfloat16 [1536, 2112], P('path'), may hold values from -6 to 6
- out_grad: bfloat16 [1536, 2112], P('path'), may hold values from -0.059814453 to 0.059814453
- doc_lengths: int32 [8, 24], P('path'), may hold values from 1 to 16, 192 in all within a row
- doc_paths: int32 [8, 24], P('path'), may hold values from 0 to 7
- membership: int32 [8, 2], replicated, may hold values from 0 to 3
- up_master: float32 [4, 2112, 8192], P(None, 'path', 'shard'), may hold values from -0.9574271 to 0.9574271
- down_master: float32 [4, 2112, 8192], P(None, 'path', 'shard'), may hold values from -0.4861359 to 0.4861359
- up_moment: bfloat16 [4, 2112, 8192], P(None, 'path', 'shard'), may hold values from -0.059814453 to 0.059814453
- down_moment: bfloat16 [4, 2112, 8192], P(None, 'path', 'shard'), may hold values from -0.059814453 to 0.059814453
Outputs:
- new_up_master: float32 [4, 2112, 8192], P(None, 'path', 'shard')
- new_down_master: float32 [4, 2112, 8192], P(None, 'path', 'shard')
- new_up_moment: bfloat16 [4, 2112, 8192], P(None, 'path', 'shard')
- new_down_moment: bfloat16 [4, 2112, 8192], P(None, 'path', 'shard')
All inputs are finite; a program needn't handle non-finite values.
Results may differ from a plain program's by a relative error of at most 0.005.
The roundings to bfloat16 on the way count: a program that leaves them out, or rounds other values in their place, can miss the bound.
Values may be sent and summed in bfloat16 or wider, within the bound.
No kernel may reach another device: no remote copies, remote signals or barrier semaphores. Data moves between devices by JAX's collectives and lax.ppermute only.
A program may use at most 128 MiB of HBM per device.

v0:
```python
import jax
import jax.numpy as jnp
from jax import lax
from jax.sharding import PartitionSpec as P

FF = 8192


norm_epsilon = 1e-06
hidden_epsilon = 1e-05
adam_epsilon = 0.001
inner_rate = 0.05
decay_rate = 0.1
outer_rate = 0.7
momentum_coef = 0.9
gelu_coef = 0.7978845608
cubic_coef = 0.044715


def gelu_pair(values):
    inner = gelu_coef * (values + cubic_coef * values * values * values)
    tangent = jnp.tanh(inner)
    activated = 0.5 * values * (1.0 + tangent)
    slopes = 0.5 * (1.0 + tangent) + 0.5 * values * (1.0 - tangent * tangent) * gelu_coef * (
        1.0 + 3.0 * cubic_coef * values * values
    )
    return (activated, slopes)


def placing_matrix(lengths, targets, row_count, path_count, capacity):
    ends = jnp.cumsum(lengths)
    row_ids = jnp.arange(row_count, dtype=jnp.int32)
    doc_of_row = jnp.sum((row_ids[:, None] >= ends[None, :]).astype(jnp.int32), axis=1)
    doc_hit = doc_of_row[:, None] == jnp.arange(lengths.shape[0], dtype=jnp.int32)[None, :]
    row_path = jnp.sum(jnp.where(doc_hit, targets[None, :], 0), axis=1)
    path_hit = (row_path[:, None] == jnp.arange(path_count, dtype=jnp.int32)[None, :]).astype(
        jnp.int32
    )
    ranks = jnp.sum((jnp.cumsum(path_hit, axis=0) - 1) * path_hit, axis=1)
    slots = jnp.where(ranks < capacity, row_path * capacity + ranks, -1)
    return (jnp.arange(path_count * capacity, dtype=jnp.int32)[:, None] == slots[None, :]).astype(
        jnp.bfloat16
    )


def adam_delta(gradient, weight):
    update = gradient / (jnp.abs(gradient) + adam_epsilon) + decay_rate * weight.astype(jnp.float32)
    return (-inner_rate * update).astype(jnp.bfloat16)


def outer_update(master, moment, summed, counts):
    pseudo = -summed / jnp.maximum(counts, 1.0)[:, None, None]
    buffer = momentum_coef * moment.astype(jnp.float32) + pseudo
    return (master - outer_rate * (pseudo + momentum_coef * buffer), buffer.astype(jnp.bfloat16))


def on_device(
    tokens,
    out_grad,
    doc_lengths,
    doc_paths,
    membership,
    up_master,
    down_master,
    up_moment,
    down_moment,
):
    path_count = lax.axis_size("path")
    row_count = tokens.shape[0]
    module_count = up_master.shape[0]
    owner_rows = up_master.shape[1]
    half_width = up_master.shape[2] // 2
    capacity = row_count // path_count
    placing = placing_matrix(doc_lengths[0], doc_paths[0], row_count, path_count, capacity)
    sent_rows = jnp.dot(placing, tokens, preferred_element_type=jnp.float32).astype(jnp.bfloat16)
    sent_grads = jnp.dot(placing, out_grad, preferred_element_type=jnp.float32).astype(jnp.bfloat16)
    rows_in, grads_in = (
        lax.all_to_all(sent_rows, "path", split_axis=0, concat_axis=0, tiled=True),
        lax.all_to_all(sent_grads, "path", split_axis=0, concat_axis=0, tiled=True),
    )
    masters = (up_master, down_master)
    moments = (up_moment, down_moment)

    def fetch(which_level):
        table_column = membership[:, which_level]
        halves = []
        for half_index in range(2):
            piece = masters[which_level][
                :, :, half_index * half_width : (half_index + 1) * half_width
            ].astype(jnp.bfloat16)
            outgoing = jnp.take(piece, table_column, axis=0)
            incoming = lax.all_to_all(outgoing, "path", split_axis=0, concat_axis=1, tiled=True)
            halves.append(incoming[0])
        return jnp.concatenate(halves, axis=1)

    def ship(which_level, gradient, weight):
        delta = adam_delta(gradient, weight)
        table_column = membership[:, which_level]
        selector = jnp.arange(module_count, dtype=jnp.int32)[:, None] == table_column[None, :]
        counts = jnp.sum(selector.astype(jnp.float32), axis=1)
        selector_b = selector.astype(jnp.bfloat16)
        summed_halves = []
        for half_index in range(2):
            outgoing = delta[:, half_index * half_width : (half_index + 1) * half_width].reshape(
                path_count, owner_rows, half_width
            )
            incoming = lax.all_to_all(outgoing, "path", split_axis=0, concat_axis=0, tiled=True)
            summed = jnp.dot(
                selector_b,
                incoming.reshape(path_count, owner_rows * half_width),
                preferred_element_type=jnp.float32,
            )
            summed_halves.append(summed.reshape(module_count, owner_rows, half_width))
        summed_all = jnp.concatenate(summed_halves, axis=2)
        return outer_update(masters[which_level], moments[which_level], summed_all, counts)

    up_weight = fetch(0)
    down_weight = fetch(1)
    rows_float = rows_in.astype(jnp.float32)
    normed = (
        rows_float
        * lax.rsqrt(jnp.mean(rows_float * rows_float, axis=1, keepdims=True) + norm_epsilon)
    ).astype(jnp.bfloat16)
    pre = jnp.dot(normed, up_weight, preferred_element_type=jnp.float32)
    activated, slopes = gelu_pair(pre)
    squares = lax.psum(jnp.sum(activated * activated, axis=1), "shard")
    scale = jnp.sqrt(squares / FF + hidden_epsilon)[:, None]
    hidden = activated / scale
    hidden_b = hidden.astype(jnp.bfloat16)
    grad_down = jnp.dot(grads_in.T, hidden_b, preferred_element_type=jnp.float32)
    back = jnp.dot(grads_in, down_weight, preferred_element_type=jnp.float32)
    products = lax.psum(jnp.sum(back * hidden, axis=1), "shard")
    mixing = (products / FF)[:, None]
    dpre = ((back - hidden * mixing) / scale * slopes).astype(jnp.bfloat16)
    grad_up = jnp.dot(normed.T, dpre, preferred_element_type=jnp.float32)
    up_result = ship(0, grad_up, up_weight)
    down_result = ship(1, grad_down, down_weight)
    return (up_result[0], down_result[0], up_result[1], down_result[1])


def solution(mesh):
    return jax.shard_map(
        on_device,
        mesh=mesh,
        in_specs=(
            P("path", None),
            P("path", None),
            P("path", None),
            P("path", None),
            P(),
            P(None, "path", "shard"),
            P(None, "path", "shard"),
            P(None, "path", "shard"),
            P(None, "path", "shard"),
        ),
        out_specs=(
            P(None, "path", "shard"),
            P(None, "path", "shard"),
            P(None, "path", "shard"),
            P(None, "path", "shard"),
        ),
        check_vma=False,
    )
```

profile of v0, /device:TPU:0, one launch (start us, length us, event | category | flops | bytes accessed | tf_op | source)
XLA Modules:
  0.0 946.1 jit_solution(5085274476432971255)
XLA Ops:
  0.6 0.0 copy-start
  0.6 0.8 copy.31
  1.5 0.1 reduce.1
  1.6 0.1 convert_reduce_fusion
  1.7 0.7 select_reduce_fusion
  2.5 0.6 reduce-window.19
  3.1 0.2 slice_reduce_fusion
  3.3 0.1 add_bitcast_fusion
  3.5 1.3 convolution_convert_fusion
  4.7 7.3 all-to-all-start.1
  12.0 0.0 copy-start.6
  12.0 6.3 convert.16
  18.3 1.3 convolution_convert_fusion.1
  19.6 13.7 %all-to-all-done.1 = bf16[8,24,2112]{2,1,0:T(8,128)(2,1)S(1)} async-done(((bf16[8,24,2112]{2,1,0:T(8,128)(2,1)}), bf16[8,24,2112]{2,1,0:T(8,128)(2,1)S(1)}, u32[]{:S(2)}, u32[]{:S(2)}) %all-to-all-start.1) | async-done | bytes 811040 | tf_op jit(solution)/shard_map/all_to_all | solution.py:79
  33.3 3.5 all-to-all-start
  36.9 4.2 fusion.51
  41.1 4.5 gather_fusion.2
  45.6 2.9 gather_fusion.3
  48.5 7.9 broadcast_select_fusion.1
  56.4 1.9 all-to-all-done
  58.2 100.5 %all_to_all.77 = bf16[8,264,1024]{2,1,0:T(8,128)(2,1)} all-to-all(bf16[8,264,1024]{2,1,0:T(8,128)(2,1)} %get-tuple-element.39), channel_id=1, replica_groups=mesh['path'=8,'shard'=4] {'path'}, dimensions={0} | all-to-all | bytes 8650752 | tf_op jit(solution)/shard_map/all_to_all | solution.py:92
  158.8 4.6 all-to-all-start.5
  163.3 4.1 convert.15
  167.5 1.8 fusion.50
  169.3 4.5 gather_fusion
  173.8 2.9 gather_fusion.1
  176.6 7.9 broadcast_select_fusion.3
  184.5 73.4 %all-to-all-done.5 = bf16[8,264,1024]{2,1,0:T(8,128)(2,1)} async-done(((bf16[8,264,1024]{2,1,0:T(8,128)(2,1)}), bf16[8,264,1024]{2,1,0:T(8,128)(2,1)}, u32[]{:S(2)}, u32[]{:S(2)}) %all-to-all-start.5) | async-done | bytes 4325408 | tf_op jit(solution)/shard_map/all_to_all | solution.py:92
  257.9 100.6 %all_to_all.78 = bf16[8,264,1024]{2,1,0:T(8,128)(2,1)} all-to-all(bf16[8,264,1024]{2,1,0:T(8,128)(2,1)} %get-tuple-element.37), channel_id=1, replica_groups=mesh['path'=8,'shard'=4] {'path'}, dimensions={0} | all-to-all | bytes 8650752 | tf_op jit(solution)/shard_map/all_to_all | solution.py:92
  358.5 4.6 all-to-all-start.3
  363.1 0.2 multiply_reduce_fusion
  363.3 0.1 rsqrt.12
  363.4 0.2 fusion.6
  363.6 0.0 copy-start.5
  363.6 6.1 multiply_reduce_fusion.2
  369.7 6.5 psum.14
  376.3 81.4 %all-to-all-done.3 = bf16[8,264,1024]{2,1,0:T(8,128)(2,1)} async-done(((bf16[8,264,1024]{2,1,0:T(8,128)(2,1)}), bf16[8,264,1024]{2,1,0:T(8,128)(2,1)}, u32[]{:S(2)}, u32[]{:S(2)}) %all-to-all-start.3) | async-done | bytes 4325408 | tf_op jit(solution)/shard_map/all_to_all | solution.py:92
  457.7 0.0 copy-done.5
  457.7 9.8 %multiply_convert_fusion = bf16[2112,2048]{1,0:T(8,128)(2,1)S(1)} fusion(bf16[192,2112]{1,0:T(8,128)(2,1)S(1)} %bitcast.93, bf16[2112,1024]{1,0:T(8,128)(2,1)} %bitcast.13, bf16[2112,1024]{1,0:T(8,128)(2,1)} %bitcast.91, f32[192]{0:T(256)S(1)} %add_sqrt_fusion, f32[192,2048]{1,0:T(8,128)S(1)} %get-tuple-element.42), kind=kOutput, calls=%fused_computation.4 | convolution fusion | flops 1712455680 | bytes 19686144 | tf_op jit(solution)/shard_map/dot_general | solution.py:130
  467.5 2.5 fusion.48
  470.1 100.0 %all_to_all.79 = bf16[8,264,1024]{2,1,0:T(8,128)(2,1)} all-to-all(bf16[8,264,1024]{2,1,0:T(8,128)(2,1)S(1)} %bitcast.88), channel_id=1, replica_groups=mesh['path'=8,'shard'=4] {'path'}, dimensions={0} | all-to-all | bytes 8650752 | tf_op jit(solution)/shard_map/all_to_all | solution.py:107
  570.1 4.6 all-to-all-start.8
  574.7 7.0 multiply_reduce_fusion.1
  581.6 6.0 psum.15
  587.7 11.0 %multiply_convert_fusion.1 = bf16[2112,2048]{1,0:T(8,128)(2,1)S(1)} fusion(bf16[192,2112]{1,0:T(8,128)(2,1)S(1)} %fusion.6, bf16[2112,1024]{1,0:T(8,128)(2,1)} %bitcast.15, bf16[2112,1024]{1,0:T(8,128)(2,1)} %bitcast.90, f32[192,2048]{1,0:T(8,128)S(1)} %get-tuple-element.42, f32[192,2048]{1,0:T(8,128)} %get-tuple-element.44, ...), kind=kOutput, calls=%fused_computation.5 | convolution fusion | flops 1717960704 | bytes 21259776 | tf_op jit(solution)/shard_map/dot_general | solution.py:135
  598.6 3.9 fusion.49
  602.5 66.8 %all-to-all-done.8 = bf16[8,264,1024]{2,1,0:T(8,128)(2,1)} async-done(((bf16[8,264,1024]{2,1,0:T(8,128)(2,1)}), bf16[8,264,1024]{2,1,0:T(8,128)(2,1)}, u32[]{:S(2)}, u32[]{:S(2)}) %all-to-all-start.8) | async-done | bytes 4325408 | tf_op jit(solution)/shard_map/all_to_all | solution.py:107
  669.3 100.5 %all_to_all.80 = bf16[8,264,1024]{2,1,0:T(8,128)(2,1)} all-to-all(bf16[8,264,1024]{2,1,0:T(8,128)(2,1)} %bitcast.87), channel_id=1, replica_groups=mesh['path'=8,'shard'=4] {'path'}, dimensions={0} | all-to-all | bytes 8650752 | tf_op jit(solution)/shard_map/all_to_all | solution.py:107
  769.9 4.9 all-to-all-start.6
  774.8 0.1 convert_reduce_fusion.1
  774.9 0.0 slice-start.3
  774.9 7.3 fusion.33
  782.2 7.2 fusion.35
  789.4 4.9 fusion.29
  794.4 74.8 %all-to-all-done.6 = bf16[8,264,1024]{2,1,0:T(8,128)(2,1)} async-done(((bf16[8,264,1024]{2,1,0:T(8,128)(2,1)}), bf16[8,264,1024]{2,1,0:T(8,128)(2,1)}, u32[]{:S(2)}, u32[]{:S(2)}) %all-to-all-start.6) | async-done | bytes 4325408 | tf_op jit(solution)/shard_map/all_to_all | solution.py:107
  869.1 5.7 fusion.31
  874.8 0.0 copy-done.2
  874.8 17.5 %fusion.3 = (bf16[4,264,2048]{2,0,1:T(4,128)(2,1)}, f32[4,264,2048]{2,0,1:T(4,128)S(1)}) fusion(bf16[4,264,2048]{2,1,0:T(8,128)(2,1)} %param.18, f32[4]{0:T(128)S(1)} %broadcast_maximum_fusion.1, f32[4,264,1024]{2,0,1:T(4,128)S(1)} %copy-done.2, f32[4,264,1024]{2,0,1:T(4,128)S(1)} %fusion.31, f32[4,264,2048]{2,1,0:T(8,128)} %param.16), kind=kLoop, calls=%fused_computation.17 | loop fusion | flops 23789568 | bytes 34603024 | tf_op jit(solution)/shard_map/convert_element_type | solution.py:54
  892.3 6.6 copy.38
  899.0 0.0 slice-done.1
  899.0 23.3 %fusion.2 = (bf16[4,264,2048]{2,0,1:T(4,128)(2,1)}, f32[4,264,2048]{2,0,1:T(4,128)S(1)}) fusion(bf16[4,264,2048]{2,1,0:T(8,128)(2,1)} %param.19, f32[4]{0:T(128)S(1)} %broadcast_maximum_fusion, f32[4,264,1024]{2,0,1:T(4,128)} %fusion.33, f32[4,264,1024]{2,0,1:T(4,128)} %fusion.35, f32[4,264,2048]{2,1,0:T(8,128)S(1)} %bitcast.80), kind=kLoop, calls=%fused_computation.15 | loop fusion | flops 23789568 | bytes 34603024 | tf_op jit(solution)/shard_map/convert_element_type | solution.py:54
  922.3 6.6 copy.39
  928.9 8.5 copy.37
  937.4 8.5 copy.36
  (37 shorter events, 0.2 us)
Async XLA Ops:
  0.6 2.8 copy-start
  4.7 28.6 %all-to-all-start.1 = ((bf16[8,24,2112]{2,1,0:T(8,128)(2,1)}), bf16[8,24,2112]{2,1,0:T(8,128)(2,1)S(1)}, u32[]{:S(2)}, u32[]{:S(2)}) async-start(bf16[8,24,2112]{2,1,0:T(8,128)(2,1)} %bitcast.9), calls=%async_computation.1 | async-start | bytes 1671168 | tf_op jit(solution)/shard_map/all_to_all | solution.py:79
  12.0 6.3 copy-start.3
  12.0 24.8 %copy-start.6 = (s32[8,2]{0,1:T(2,128)S(1)}, s32[8,2]{0,1:T(2,128)}, u32[]{:S(2)}) copy-start(s32[8,2]{0,1:T(2,128)} %param.15) | copy-start | bytes 196
  33.3 3.6 copy-start.4
  33.3 24.9 %all-to-all-start = ((bf16[8,24,2112]{2,1,0:T(8,128)(2,1)}), bf16[8,24,2112]{2,1,0:T(8,128)(2,1)S(1)}, u32[]{:S(2)}, u32[]{:S(2)}) async-start(bf16[8,24,2112]{2,1,0:T(8,128)(2,1)} %bitcast.7), calls=%async_computation | async-start | bytes 1671168 | tf_op jit(solution)/shard_map/all_to_all | solution.py:78
  158.8 99.1 %all-to-all-start.5 = ((bf16[8,264,1024]{2,1,0:T(8,128)(2,1)}), bf16[8,264,1024]{2,1,0:T(8,128)(2,1)}, u32[]{:S(2)}, u32[]{:S(2)}) async-start(bf16[8,264,1024]{2,1,0:T(8,128)(2,1)} %get-tuple-element.40), calls=%async_computation.5 | async-start | bytes 8650752 | tf_op jit(solution)/shard_map/all_to_all | solution.py:92
  358.5 99.2 %all-to-all-start.3 = ((bf16[8,264,1024]{2,1,0:T(8,128)(2,1)}), bf16[8,264,1024]{2,1,0:T(8,128)(2,1)}, u32[]{:S(2)}, u32[]{:S(2)}) async-start(bf16[8,264,1024]{2,1,0:T(8,128)(2,1)} %get-tuple-element.38), calls=%async_computation.3 | async-start | bytes 8650752 | tf_op jit(solution)/shard_map/all_to_all | solution.py:92
  363.6 94.1 %copy-start.5 = (bf16[8,24,2112]{2,1,0:T(8,128)(2,1)S(1)}, bf16[8,24,2112]{2,1,0:T(8,128)(2,1)}, u32[]{:S(2)}) copy-start(bf16[8,24,2112]{2,1,0:T(8,128)(2,1)} %copy-done.4) | copy-start | bytes 2433028
  570.1 99.3 %all-to-all-start.8 = ((bf16[8,264,1024]{2,1,0:T(8,128)(2,1)}), bf16[8,264,1024]{2,1,0:T(8,128)(2,1)}, u32[]{:S(2)}, u32[]{:S(2)}) async-start(bf16[8,264,1024]{2,1,0:T(8,128)(2,1)} %bitcast.86), calls=%async_computation.8 | async-start | bytes 8650752 | tf_op jit(solution)/shard_map/all_to_all | solution.py:107
  769.9 4.9 copy-start.7
  769.9 99.3 %all-to-all-start.6 = ((bf16[8,264,1024]{2,1,0:T(8,128)(2,1)}), bf16[8,264,1024]{2,1,0:T(8,128)(2,1)}, u32[]{:S(2)}, u32[]{:S(2)}) async-start(bf16[8,264,1024]{2,1,0:T(8,128)(2,1)} %bitcast.85), calls=%async_computation.6 | async-start | bytes 8650752 | tf_op jit(solution)/shard_map/all_to_all | solution.py:107
  774.9 14.5 %slice-start.3 = ((s8[4325376]{0:T(1024)(128)(4,1)}), s8[4194304]{0:T(1024)(128)(4,1)S(1)}, s32[]{:S(2)}) async-start(s8[4325376]{0:T(1024)(128)(4,1)} %bitcast.82), calls=%async_computation.13 | async-start | bytes 8388608
  782.2 7.2 slice-start.4
  869.1 5.7 copy-start.2
  869.1 29.8 %slice-start = ((s8[8650752]{0:T(1024)(128)(4,1)}), s8[4194304]{0:T(1024)(128)(4,1)S(1)}, s32[]{:S(2)}) async-start(s8[8650752]{0:T(1024)(128)(4,1)} %bitcast.79), calls=%async_computation.10 | async-start | bytes 8388608
  874.8 24.2 %slice-start.1 = ((s8[8650752]{0:T(1024)(128)(4,1)}), s8[4194304]{0:T(1024)(128)(4,1)S(1)}, s32[]{:S(2)}) async-start(s8[8650752]{0:T(1024)(128)(4,1)} %bitcast.79), calls=%async_computation.11 | async-start | bytes 8388608
  874.8 24.2 %slice-start.2 = ((s8[8650752]{0:T(1024)(128)(4,1)}), s8[262144]{0:T(1024)(128)(4,1)S(1)}, s32[]{:S(2)}) async-start(s8[8650752]{0:T(1024)(128)(4,1)} %bitcast.79), calls=%async_computation.12 | async-start | bytes 524288
  937.4 8.5 copy-start.1
where the time goes:
time: 954 us; the launch traced here: 946 us
  blocking collectives  414 us (43%)
  waiting for transfers between devices  312 us (33%)
  other arithmetic  69.3 us (7%)
  matrix products  61.5 us (6%)
  local copies, waits for them, and re-layouts  58.7 us (6%)
  starting transfers between devices  29.4 us (3%)
    all_to_all x2, blocking collectives, fetch(): lax.all_to_all(outgoing, 'path', split_axis=0, concat_axis=1, tiled=True)  201 us
    all_to_all x2, blocking collectives, ship(): lax.all_to_all(outgoing, 'path', split_axis=0, concat_axis=0, tiled=True)  201 us
    all_to_all x2, waiting for transfers between devices, fetch(): lax.all_to_all(outgoing, 'path', split_axis=0, concat_axis=1, tiled=True)  155 us
    all_to_all x2, waiting for transfers between devices, ship(): lax.all_to_all(outgoing, 'path', split_axis=0, concat_axis=0, tiled=True)  142 us
    convert_element_type x2, other arithmetic, outer_update(): buffer.astype(jnp.bfloat16)  40.8 us
    unnamed x30, local copies, waits for them, and re-layouts  30.3 us
    dot_general x4, matrix products, ship(): jnp.dot(selector_b, incoming.reshape(path_count, owner_rows * half_width)...  25.1 us
  transfers between devices with their start and end apart: 6, of which 6 were waited for; matrix products, arithmetic and copies ran while one was open for 10% of the time, Pallas kernels for 0%

commit v1 on v0

v1 whole, which is shorter than its diff:
```python
import functools

import jax
import jax.numpy as jnp
from jax import lax
from jax.experimental import pallas as pl
from jax.experimental.pallas import tpu as pltpu
from jax.sharding import PartitionSpec as P

norm_epsilon = 1e-06
hidden_epsilon = 1e-05
adam_epsilon = 0.001
inner_rate = 0.05
decay_rate = 0.1
outer_rate = 0.7
momentum_coef = 0.9
vmem_limit = 56 * 1024 * 1024
small_cost = pl.CostEstimate(flops=1, bytes_accessed=1, transcendentals=0)
gelu_coef = 0.7978845608
cubic_coef = 0.044715


def gelu_pair(values):
    inner = gelu_coef * (values + cubic_coef * values * values * values)
    tangent = jnp.tanh(inner)
    activated = 0.5 * values * (1.0 + tangent)
    slopes = 0.5 * (1.0 + tangent) + 0.5 * values * (1.0 - tangent * tangent) * gelu_coef * (
        1.0 + 3.0 * cubic_coef * values * values
    )
    return (activated, slopes)


def placing_matrix(lengths, targets, row_count, path_count, capacity, first_slot, slot_count):
    ends = jnp.cumsum(lengths)
    row_ids = jnp.arange(row_count, dtype=jnp.int32)
    doc_of_row = jnp.sum((row_ids[:, None] >= ends[None, :]).astype(jnp.int32), axis=1)
    doc_hit = doc_of_row[:, None] == jnp.arange(lengths.shape[0], dtype=jnp.int32)[None, :]
    row_path = jnp.sum(jnp.where(doc_hit, targets[None, :], 0), axis=1)
    path_hit = (row_path[:, None] == jnp.arange(path_count, dtype=jnp.int32)[None, :]).astype(
        jnp.int32
    )
    ranks = jnp.sum((jnp.cumsum(path_hit, axis=0) - 1) * path_hit, axis=1)
    slots = jnp.where(ranks < capacity, row_path * capacity + ranks, -1)
    wanted = first_slot + jnp.arange(slot_count, dtype=jnp.int32)
    return (wanted[:, None] == slots[None, :]).astype(jnp.bfloat16)


def outgoing_kernel(table_ref, *refs):
    half = len(refs) // 2
    for master_ref, out_ref in zip(refs[:half], refs[half:]):
        out_ref[...] = master_ref[...].astype(jnp.bfloat16)


def outgoing_weights(member, team, master):
    count, owned, width = master.shape
    block = width // team
    masks = range(1, team)
    return pl.pallas_call(
        outgoing_kernel,
        out_shape=[jax.ShapeDtypeStruct((count, owned, block), jnp.bfloat16) for _ in masks],
        grid_spec=pltpu.PrefetchScalarGridSpec(
            num_scalar_prefetch=1,
            grid=(count,),
            in_specs=[
                pl.BlockSpec((1, owned, block), lambda i, t, mask=mask: (i, 0, t[0] ^ mask))
                for mask in masks
            ],
            out_specs=[pl.BlockSpec((1, owned, block), lambda i, t: (i, 0, 0)) for _ in masks],
        ),
        compiler_params=pltpu.CompilerParams(vmem_limit_bytes=vmem_limit),
        cost_estimate=small_cost,
        name="outgoing_weights",
    )(member.reshape(1), *[master for _ in masks])


def arranged_kernel(team, table_ref, *refs):
    pieces, (out_ref, by_source_ref, rows_ref) = refs[: 2 * team], refs[2 * team :]
    member, group, quarter = table_ref[0], table_ref[1], table_ref[2]
    _, groups, _, _, capacity, _ = pieces[0].shape
    sources = groups * team
    owned = out_ref.shape[3]

    def collect(half):
        for mask in range(team):
            for offset in range(groups):
                source = lax.rem(group + groups - offset, groups) * team + (member ^ mask)
                by_source_ref[source] = half[mask][0, offset, 0, 0].astype(jnp.float32)

    mine = ((pl.program_id(0) // (pl.num_programs(0) // 4)) ^ quarter) % 2 == 0

    @pl.when(mine)
    def _():
        collect(pieces[:team])

    @pl.when(jnp.logical_not(mine))
    def _():
        collect(pieces[team:])

    for source in range(sources):
        rows_ref[source * capacity : (source + 1) * capacity, :] = by_source_ref[source]
    for block in range(team):
        out_ref[0, block] = rows_ref[:, block * owned : (block + 1) * owned].astype(jnp.bfloat16)


def arranged(which, table, team, paths, mine, theirs):
    _, groups, _, kept, capacity, depth = mine[0].shape
    slots = paths * capacity
    owned = depth // team
    piece = pl.BlockSpec(
        (1, groups, 1, 1, capacity, depth),
        lambda p, t: ((lax.div(p, kept) ^ t[2]) // 2, 0, which, lax.rem(p, kept), 0, 0),
    )
    return pl.pallas_call(
        functools.partial(arranged_kernel, team),
        out_shape=jax.ShapeDtypeStruct((paths, team, slots, owned), jnp.bfloat16),
        grid_spec=pltpu.PrefetchScalarGridSpec(
            num_scalar_prefetch=1,
            grid=(paths,),
            in_specs=[piece] * (2 * team),
            out_specs=pl.BlockSpec((1, team, slots, owned), lambda p, t: (p, 0, 0, 0)),
            scratch_shapes=[
                pltpu.VMEM((groups * team, capacity, depth), jnp.float32),
                pltpu.VMEM((slots, depth), jnp.float32),
            ],
        ),
        compiler_params=pltpu.CompilerParams(vmem_limit_bytes=vmem_limit),
        cost_estimate=small_cost,
        name="arranged",
    )(table, *mine, *theirs)


def product_kernel(team, listed, table_ref, rows_ref, own_ref, *refs):
    received, out_ref = refs[:-1], refs[-1]
    member = table_ref[0]
    module = table_ref[1 + listed + pl.program_id(0)]
    total = jnp.dot(
        rows_ref[0, member],
        own_ref[module].astype(jnp.bfloat16),
        preferred_element_type=jnp.float32,
    )
    for mask in range(1, team):
        total += jnp.dot(
            rows_ref[0, member ^ mask],
            received[mask - 1][module],
            preferred_element_type=jnp.float32,
        )
    out_ref[0] = total


def products(member, paths, modules, rows, master, received):
    _, team, slots, owned = rows.shape
    count, _, block = received[0].shape
    listed = paths.shape[0]
    table = jnp.concatenate([member.reshape(1), paths, jnp.take(modules, paths)])
    weights = pl.BlockSpec((count, owned, block), lambda i, t: (0, 0, 0))
    return pl.pallas_call(
        functools.partial(product_kernel, team, listed),
        out_shape=jax.ShapeDtypeStruct((listed, slots, block), jnp.float32),
        grid_spec=pltpu.PrefetchScalarGridSpec(
            num_scalar_prefetch=1,
            grid=(listed,),
            in_specs=[
                pl.BlockSpec((1, team, slots, owned), lambda i, t: (t[1 + i], 0, 0, 0)),
                pl.BlockSpec((count, owned, block), lambda i, t: (0, 0, t[0])),
            ]
            + [weights] * (team - 1),
            out_specs=pl.BlockSpec((1, slots, block), lambda i, t: (i, 0, 0)),
        ),
        compiler_params=pltpu.CompilerParams(vmem_limit_bytes=vmem_limit),
        cost_estimate=small_cost,
        name="products",
    )(table, rows, master, *received)


def update_kernel(blocks, groups, tiles, previous_count, table_ref, left_ref, *refs):
    rights = refs[: blocks * groups]
    master_ref, moment_ref = refs[blocks * groups : blocks * groups + 2]
    new_master_ref, new_moment_ref, sums_ref, decay_ref = refs[blocks * groups + 2 + previous_count :]
    paths = left_ref.shape[0]
    sums_ref[...] = jnp.zeros_like(sums_ref)
    decay_ref[...] = decay_rate * master_ref[...].astype(jnp.bfloat16).astype(jnp.float32)

    def accumulate(block):
        for group in range(groups):
            right_ref = rights[block * groups + group]
            for member in range(right_ref.shape[0]):
                path = table_ref[blocks + group] + member
                module = table_ref[blocks + groups + path]
                gradient = jnp.dot(
                    left_ref[path], right_ref[member], preferred_element_type=jnp.float32
                )
                step = gradient * pl.reciprocal(jnp.abs(gradient) + adam_epsilon)
                update = step + decay_ref[module]
                sums_ref[module] += (-inner_rate * update).astype(jnp.bfloat16).astype(jnp.float32)

    for block in range(blocks):
        pl.when(pl.program_id(0) // tiles == block)(functools.partial(accumulate, block))

    for module in range(master_ref.shape[0]):
        count = lax.fori_loop(
            0,
            paths,
            lambda path, total: total
            + (table_ref[blocks + groups + path] == module).astype(jnp.int32),
            0,
        )
        divisor = jnp.maximum(count, 1).astype(jnp.float32)
        pseudo = -sums_ref[module] / divisor
        buffer = momentum_coef * moment_ref[module].astype(jnp.float32) + pseudo
        new_master_ref[module] = master_ref[module] - outer_rate * (pseudo + momentum_coef * buffer)
        new_moment_ref[module] = buffer.astype(jnp.bfloat16)


def updated(columns, firsts, modules, left, rights, master, moment, previous):
    paths, owned, slots = left.shape
    count, _, width = master.shape
    blocks, groups = len(rights), len(rights[0])
    members, _, block = rights[0][0].shape
    tile = min(256, block)
    tiles = block // tile
    table = jnp.concatenate([jnp.stack(columns), firsts, modules])
    module_spec = pl.BlockSpec(
        (count, owned, tile),
        lambda f, t: (0, 0, t[lax.div(f, tiles)] * tiles + lax.rem(f, tiles)),
    )
    right_specs = [
        pl.BlockSpec(
            (members, slots, tile),
            lambda f, t, start=index * tiles: (0, 0, jnp.clip(f - start, 0, tiles - 1)),
        )
        for index in range(blocks)
        for _ in range(groups)
    ]
    first_previous = 4 + blocks * groups
    return pl.pallas_call(
        functools.partial(update_kernel, blocks, groups, tiles, len(previous)),
        out_shape=(
            jax.ShapeDtypeStruct(master.shape, jnp.float32),
            jax.ShapeDtypeStruct(master.shape, jnp.bfloat16),
        ),
        grid_spec=pltpu.PrefetchScalarGridSpec(
            num_scalar_prefetch=1,
            grid=(blocks * tiles,),
            in_specs=[pl.BlockSpec((paths, owned, slots), lambda f, t: (0, 0, 0))]
            + right_specs
            + [module_spec, module_spec]
            + [pl.BlockSpec(memory_space=pl.ANY)] * len(previous),
            out_specs=[module_spec, module_spec],
            scratch_shapes=[pltpu.VMEM((count, owned, tile), jnp.float32)] * 2,
        ),
        input_output_aliases={first_previous + i: i for i in range(len(previous))},
        compiler_params=pltpu.CompilerParams(vmem_limit_bytes=vmem_limit),
        cost_estimate=small_cost,
        name="updated",
    )(table, left, *[right for listed in rights for right in listed], master, moment, *previous)


def on_device(
    tokens,
    out_grad,
    doc_lengths,
    doc_paths,
    membership,
    up_master,
    down_master,
    up_moment,
    down_moment,
):
    path_count = lax.axis_size("path")
    shard_count = lax.axis_size("shard")
    row_count, features = tokens.shape
    width = up_master.shape[2]
    hidden_units = width * shard_count
    capacity = row_count // path_count
    slots = path_count * capacity
    kept = path_count // 4
    up_modules, down_modules = membership[:, 0], membership[:, 1]

    team = 4
    groups = path_count // team
    me = lax.axis_index("path")
    member, group = me % team, me // team
    quarter = lax.axis_index("shard") % 4
    bits = (2, 1)

    def trade(value, mask):
        return lax.ppermute(value, "path", [(i, i ^ mask) for i in range(path_count)])

    def move(value, offset):
        if offset == 0:
            return value
        return lax.ppermute(
            value, "path", [(i, (i + team * offset) % path_count) for i in range(path_count)]
        )

    def share(value, mask):
        return lax.ppermute(value, "shard", [(i, i ^ mask) for i in range(shard_count)])

    def tie(*values):
        return lax.optimization_barrier(values)

    up_out = outgoing_weights(member, team, up_master)
    up_beside, up_near = trade(up_out[0], 1), trade(up_out[1], 2)

    placing = placing_matrix(
        doc_lengths[0],
        doc_paths[0],
        row_count,
        path_count,
        capacity,
        quarter * kept * capacity,
        kept * capacity,
    )
    rows = jnp.dot(placing, tokens, preferred_element_type=jnp.float32)
    grads = jnp.dot(placing, out_grad, preferred_element_type=jnp.float32).astype(jnp.bfloat16)
    normed = (
        rows * lax.rsqrt(jnp.mean(rows * rows, axis=1, keepdims=True) + norm_epsilon)
    ).astype(jnp.bfloat16)
    depth = features // groups

    sent = jnp.stack([normed, grads]).reshape(2, kept, capacity, features)
    pieces = jnp.stack(
        [
            move(
                lax.dynamic_slice_in_dim(sent, (group + offset) % groups * depth, depth, 3), offset
            )
            for offset in range(groups)
        ]
    )
    near, beside, along = trade(pieces, 2), trade(pieces, 1), share(pieces, 2)
    near, beside, along, up_beside, up_near, across = tie(
        near, beside, along, up_beside, up_near, up_out[2]
    )
    up_across = trade(across, 3)
    near_beside = trade(near, 1)
    near_along, beside_along = share(near, 2), share(beside, 2)
    down_out = outgoing_weights(member, team, down_master)
    near_beside, near_along, beside_along, down_out = tie(
        near_beside, near_along, beside_along, down_out
    )
    down_near = trade(down_out[1], 2)
    mine = [
        jnp.stack(pair)
        for pair in (
            (pieces, along),
            (beside, beside_along),
            (near, near_along),
            (near_beside, share(near_beside, 2)),
        )
    ]
    theirs = [share(value, 1) for value in mine]
    down_beside, down_across = trade(down_out[0], 1), trade(down_out[2], 3)
    place = jnp.stack([member, group, quarter])

    def group_paths(offset):
        return (group + offset) % groups * team + jnp.arange(team, dtype=jnp.int32)

    def part_of(offset, rows, modules, master, weights):
        return products(member, group_paths(offset), modules, rows, master, weights)

    def summed(own, moved):
        for value in moved:
            own = own + value
        return own

    others = range(1, groups)

    def row_sums(values):
        summed = lax.psum(jnp.sum(values, axis=2), "shard")
        for bit in bits:
            summed = summed + trade(summed, bit)
        return summed

    def own_blocks(block):
        return [move(block, offset) for offset in range(groups)]

    firsts = jnp.stack([(group + groups - offset) % groups * team for offset in range(groups)])
    def outer_step(found, results, some_batches, modules, left, master, moment):
        for batch in some_batches:
            results = updated(
                [member ^ mask for mask in batch],
                firsts,
                modules,
                left,
                [found[mask] for mask in batch],
                master,
                moment,
                results,
            )
        return results

    def left_of(rows):
        return lax.dynamic_index_in_dim(rows, member, 1, False).transpose(0, 2, 1)

    def moved(block):
        return [move(block, offset) for offset in others]

    normed_rows = arranged(0, place, team, path_count, mine, theirs)
    normed_rows, down_near = tie(normed_rows, down_near)
    up_operands = (normed_rows, up_modules, up_master, [up_beside, up_near, up_across])
    pre_moved = [move(part_of(offset, *up_operands), offset) for offset in others]
    pre_own = part_of(0, *up_operands)
    late_place, pre_own = tie(place, pre_own)
    grad_rows = arranged(1, late_place, team, path_count, mine, theirs)
    down_operands = (grad_rows, down_modules, down_master, [down_beside, down_near, down_across])
    back_parts = [part_of(offset, *down_operands) for offset in others]
    back_own = part_of(0, *down_operands)
    pre_moved, back_parts = tie(pre_moved, back_parts)
    early = 2
    back_early = [move(part[:early], offset) for part, offset in zip(back_parts, others)]

    activated, slopes = gelu_pair(summed(pre_own, pre_moved))
    scale = jnp.sqrt(row_sums(activated * activated) / hidden_units + hidden_epsilon)[:, :, None]
    hidden = activated / scale
    hidden, back_early = tie(hidden, back_early)
    hidden_b = hidden.astype(jnp.bfloat16)
    near, beside, far = trade(hidden_b, 2), trade(hidden_b, 1), moved(hidden_b)
    far, near, beside, back_parts, back_own = tie(far, near, beside, back_parts, back_own)
    back_late = [move(part[early:], offset) for part, offset in zip(back_parts, others)]
    far_near = [trade(value, 2) for value in far]
    far_beside = [trade(value, 1) for value in far]
    near_beside = trade(near, 1)

    def down_step(results, mask, right):
        return outer_step(
            {mask: right}, results, [[mask]], down_modules, lefts[1], down_master, down_moment
        )

    def up_step(results, mask, right):
        return outer_step(
            {mask: right}, results, [[mask]], up_modules, lefts[0], up_master, up_moment
        )

    lefts = left_of(normed_rows), left_of(grad_rows)
    down_result = down_step((), 0, [hidden_b, *far])
    far_near, far_beside, near_beside, lefts, down_result = tie(
        far_near, far_beside, near_beside, lefts, down_result
    )
    last = [trade(value, 1) for value in far_near]
    back_late, down_result = tie(back_late, down_result)

    back_moved = [jnp.concatenate(pair, axis=0) for pair in zip(back_early, back_late)]
    back = summed(back_own, back_moved)
    mixing = (row_sums(back * hidden) / hidden_units)[:, :, None]
    dpre = ((back - hidden * mixing) / scale * slopes).astype(jnp.bfloat16)
    d_far, d_near, d_beside = moved(dpre), trade(dpre, 2), trade(dpre, 1)
    down_result = down_step(down_result, 2, [near, *far_near])
    last, d_near, d_beside, down_result = tie(last, d_near, d_beside, down_result)
    d_near_beside = trade(d_near, 1)
    down_result = down_step(down_result, 1, [beside, *far_beside])
    down_result = down_step(down_result, 3, [near_beside, *last])
    d_far, d_near_beside, down_result = tie(d_far, d_near_beside, down_result)
    d_far_near = [trade(value, 2) for value in d_far]
    d_far_beside = [trade(value, 1) for value in d_far]
    up_result = up_step((), 0, [dpre, *d_far])
    d_far_beside, up_result = tie(d_far_beside, up_result)
    d_last = [trade(value, 2) for value in d_far_beside]
    up_result = up_step(up_result, 2, [d_near, *d_far_near])
    up_result = up_step(up_result, 1, [d_beside, *d_far_beside])
    up_result = up_step(up_result, 3, [d_near_beside, *d_last])
    return (up_result[0], down_result[0], up_result[1], down_result[1])


def solution(mesh):
    return jax.shard_map(
        on_device,
        mesh=mesh,
        in_specs=(
            P("path", None),
            P("path", None),
            P("path", None),
            P("path", None),
            P(),
            P(None, "path", "shard"),
            P(None, "path", "shard"),
            P(None, "path", "shard"),
            P(None, "path", "shard"),
        ),
        out_specs=(
            P(None, "path", "shard"),
            P(None, "path", "shard"),
            P(None, "path", "shard"),
            P(None, "path", "shard"),
        ),
        check_vma=False,
    )
```

time: 954 us -> 413 us (0.43)
  blocking collectives: 414 us -> 12.7 us
  waiting for transfers between devices: 312 us -> 193 us
  Pallas kernels: 0 us -> 117 us
  matrix products: 61.5 us -> 2.59 us
  other arithmetic: 69.3 us -> 20.5 us
  local copies, waits for them, and re-layouts: 58.7 us -> 19.5 us
  starting transfers between devices: 29.4 us -> 45 us
    all_to_all x4 -> x0, blocking collectives: 402 us -> none  [the longest x2 201 us: fetch(): lax.all_to_all(outgoing, 'path', split_axis=0, concat_axis=1, tiled=True)]
    all_to_all x6 -> x0, waiting for transfers between devices: 312 us -> none  [the longest x2 155 us: fetch(): lax.all_to_all(outgoing, 'path', split_axis=0, concat_axis=1, tiled=True)]
    ppermute x0 -> x39, waiting for transfers between devices: none -> 193 us  [the longest x25 135 us: trade(): lax.ppermute(value, 'path', [(i, i ^ mask) for i in range(path_count)])]
    pallas_call x0 -> x16, Pallas kernels: none -> 117 us  [the longest x8 59.9 us: updated(): pl.pallas_call(functools.partial(update_kernel, blocks, groups, tiles, le...]
    dot_general x9 -> x1, matrix products: 60.2 us -> 0.43 us  [on_device(): rows = jnp.dot(placing, tokens, preferred_element_type=jnp.float32)]
    ppermute x0 -> x39, starting transfers between devices: none -> 45 us  [the longest x25 28.1 us: trade(): lax.ppermute(value, 'path', [(i, i ^ mask) for i in range(path_count)])]
    convert_element_type x3, other arithmetic: 41 us -> 3.43 us  [the longest x1 3.24 us: on_device(): dpre = ((back - hidden * mixing) / scale * slopes).astype(jnp.bfloat16)]
    all_to_all x6 -> x0, starting transfers between devices: 29.4 us -> none  [the longest x2 9.44 us: ship(): lax.all_to_all(outgoing, 'path', split_axis=0, concat_axis=0, tiled=True)]
  transfers between devices with their start and end apart: 6 -> 39, of which waited for: 6 -> 27; matrix products, arithmetic and copies ran while one was open for 10% -> 9% of each run, Pallas kernels for 0% -> 24%
where the time goes in v1:
time: 413 us; the launch traced here: 412 us
  waiting for transfers between devices  193 us (47%)
  Pallas kernels  117 us (28%)
  starting transfers between devices  45 us (11%)
  other arithmetic  20.5 us (5%)
  local copies, waits for them, and re-layouts  19.5 us (5%)
  blocking collectives  12.7 us (3%)
    ppermute x25, waiting for transfers between devices, trade(): lax.ppermute(value, 'path', [(i, i ^ mask) for i in range(path_count)])  135 us
    pallas_call x8, Pallas kernels, updated(): pl.pallas_call(functools.partial(update_kernel, blocks, groups, tiles, le...  59.9 us
    ppermute x6, waiting for transfers between devices, move(): lax.ppermute(value, 'path', [(i, (i + team * offset) % path_count) for i...  44.3 us
    pallas_call x4, Pallas kernels, products(): pl.pallas_call(functools.partial(product_kernel, team, listed), out_shape...  28.8 us
    ppermute x25, starting transfers between devices, trade(): lax.ppermute(value, 'path', [(i, i ^ mask) for i in range(path_count)])  28.1 us
    pallas_call x2, Pallas kernels, arranged(): pl.pallas_call(functools.partial(arranged_kernel, team), out_shape=jax.Sh...  17.9 us
    ppermute x8, waiting for transfers between devices, share(): lax.ppermute(value, 'shard', [(i, i ^ mask) for i in range(shard_count)])  14.1 us
    psum x2, blocking collectives, row_sums(): summed = lax.psum(jnp.sum(values, axis=2), 'shard')  12.7 us
  transfers between devices with their start and end apart: 39, of which 27 were waited for; matrix products, arithmetic and copies ran while one was open for 9% of the time, Pallas kernels for 24%

profile of v1, /device:TPU:0, one launch (start us, length us, event | category | flops | bytes accessed | tf_op | source)
XLA Modules:
  0.0 411.5 jit_solution(12145909845367767004)
XLA Ops:
  0.7 5.0 %outgoing_weights.2 = (bf16[4,264,512]{2,1,0:T(8,128)(2,1)}, bf16[4,264,512]{2,1,0:T(8,128)(2,1)}, bf16[4,264,512]{2,1,0:T(8,128)(2,1)}) custom-call(s32[1]{0:T(128)} %bitcast.4.table_ref, f32[4,264,2048]{2,1,0:T(8,128)} %refs_2_.19, f32[4,264,2048]{2,1,0:T(8,128)} %refs_2_.19, f32[4,264,2048]{2,1,0:T(8,128)} %refs_2_.19), custom_call_target="tpu_custom_call" | custom-call | flops 1 | bytes 1 | tf_op jit(solution)/shard_map/outgoing_weights/pallas_call | solution.py:58
  5.7 3.0 collective-permute-start.4
  8.7 1.6 collective-permute-start.5
  11.7 2.2 convolution_convert_fusion
  15.6 2.7 collective-permute-start
  18.3 19.8 %collective-permute-done = bf16[2,2,24,1056]{3,2,1,0:T(8,128)(2,1)S(1)} collective-permute-done((bf16[2,2,24,1056]{3,2,1,0:T(8,128)(2,1)S(1)}, bf16[2,2,24,1056]{3,2,1,0:T(8,128)(2,1)S(1)}, u32[]{:S(2)}, u32[]{:S(2)}) %collective-permute-start) | collective-permute-done | bytes 202784 | tf_op jit(solution)/shard_map/ppermute | solution.py:292
  38.7 3.5 collective-permute-start.1
  43.7 5.3 %collective-permute-done.2 = bf16[2,2,2,24,1056]{4,3,2,1,0:T(8,128)(2,1)} collective-permute-done((bf16[2,2,2,24,1056]{4,3,2,1,0:T(8,128)(2,1)S(1)}, bf16[2,2,2,24,1056]{4,3,2,1,0:T(8,128)(2,1)}, u32[]{:S(2)}, u32[]{:S(2)}) %collective-permute-start.2) | collective-permute-done | bytes 405536 | tf_op jit(solution)/shard_map/ppermute | solution.py:287
  49.0 2.0 collective-permute-done.1
  52.4 1.6 collective-permute-start.7
  57.2 5.2 %outgoing_weights.3 = (bf16[4,264,512]{2,1,0:T(8,128)(2,1)}, bf16[4,264,512]{2,1,0:T(8,128)(2,1)}, bf16[4,264,512]{2,1,0:T(8,128)(2,1)}) custom-call(s32[1]{0:T(128)} %bitcast.4.table_ref, f32[4,264,2048]{2,1,0:T(8,128)} %refs_2_.15, f32[4,264,2048]{2,1,0:T(8,128)} %refs_2_.15, f32[4,264,2048]{2,1,0:T(8,128)} %refs_2_.15), custom_call_target="tpu_custom_call" | custom-call | flops 1 | bytes 1 | tf_op jit(solution)/shard_map/outgoing_weights/pallas_call | solution.py:58
  62.8 9.4 %collective-permute-done.8 = bf16[2,2,2,24,1056]{4,3,2,1,0:T(8,128)(2,1)} collective-permute-done((bf16[2,2,2,24,1056]{4,3,2,1,0:T(8,128)(2,1)}, bf16[2,2,2,24,1056]{4,3,2,1,0:T(8,128)(2,1)}, u32[]{:S(2)}, u32[]{:S(2)}) %collective-permute-start.8) | collective-permute-done | bytes 405536 | tf_op jit(solution)/shard_map/ppermute | solution.py:297
  75.1 2.4 pad_maximum_fusion.1.refs_1_
  77.7 3.2 collective-permute-done.9
  81.6 2.1 pad_maximum_fusion.3.refs_3_
  88.1 8.9 %arranged.2.rows_ref = bf16[8,4,192,264]{3,2,1,0:T(8,128)(2,1)} custom-call(s32[3]{0:T(128)} %pad_add_fusion.table_ref, bf16[2,2,2,2,24,1056]{5,4,3,2,1,0:T(8,128)(2,1)} %copy-done.5, bf16[2,2,2,2,24,1056]{5,4,3,2,1,0:T(8,128)(2,1)} %pad_maximum_fusion.1.refs_1_, bf16[2,2,2,2,24,1056]{5,4,3,2,1,0:T(8,128)(2,1)} %copy-done.6, ...), custom_call_target="tpu_custom_call" | custom-call | flops 1 | bytes 1 | tf_op jit(solution)/shard_map/arranged/pallas_call | solution.py:113
  97.1 14.9 %collective-permute-done.14.refs_1_ = bf16[4,264,512]{2,1,0:T(8,128)(2,1)} collective-permute-done((bf16[4,264,512]{2,1,0:T(8,128)(2,1)}, bf16[4,264,512]{2,1,0:T(8,128)(2,1)}, u32[]{:S(2)}, u32[]{:S(2)}) %collective-permute-start.14) | collective-permute-done | bytes 1081376 | tf_op jit(solution)/shard_map/ppermute | solution.py:287
  112.0 7.2 %products.5 = f32[4,192,512]{2,1,0:T(8,128)} custom-call(s32[9]{0:T(128)} %get-tuple-element.167.table_ref, bf16[8,4,192,264]{3,2,1,0:T(8,128)(2,1)} %arranged.2.rows_ref, f32[4,264,2048]{2,1,0:T(8,128)} %refs_2_.19, bf16[4,264,512]{2,1,0:T(8,128)(2,1)} %copy-done.8, bf16[4,264,512]{2,1,0:T(8,128)(2,1)} %copy-done.9, ...), custom_call_target="tpu_custom_call" | custom-call | flops 1 | bytes 1 | tf_op jit(solution)/shard_map/products/pallas_call | solution.py:156
  120.9 1.6 collective-permute-start.18
  124.4 7.1 %products.4 = f32[4,192,512]{2,1,0:T(8,128)} custom-call(s32[9]{0:T(128)} %get-tuple-element.165.table_ref, bf16[8,4,192,264]{3,2,1,0:T(8,128)(2,1)} %arranged.2.rows_ref, f32[4,264,2048]{2,1,0:T(8,128)} %refs_2_.19, bf16[4,264,512]{2,1,0:T(8,128)(2,1)} %copy-done.8, bf16[4,264,512]{2,1,0:T(8,128)(2,1)} %copy-done.9, ...), custom_call_target="tpu_custom_call" | custom-call | flops 1 | bytes 1 | tf_op jit(solution)/shard_map/products/pallas_call | solution.py:156
  131.5 8.9 %arranged.3.rows_ref = bf16[8,4,192,264]{3,2,1,0:T(8,128)(2,1)} custom-call(s32[3]{0:T(128)} %pad_add_fusion.table_ref, bf16[2,2,2,2,24,1056]{5,4,3,2,1,0:T(8,128)(2,1)} %copy-done.5, bf16[2,2,2,2,24,1056]{5,4,3,2,1,0:T(8,128)(2,1)} %pad_maximum_fusion.1.refs_1_, bf16[2,2,2,2,24,1056]{5,4,3,2,1,0:T(8,128)(2,1)} %copy-done.6, ...), custom_call_target="tpu_custom_call" | custom-call | flops 1 | bytes 1 | tf_op jit(solution)/shard_map/arranged/pallas_call | solution.py:113
  140.5 27.2 %collective-permute-done.17.refs_0_ = bf16[4,264,512]{2,1,0:T(8,128)(2,1)S(1)} collective-permute-done((bf16[4,264,512]{2,1,0:T(8,128)(2,1)}, bf16[4,264,512]{2,1,0:T(8,128)(2,1)S(1)}, u32[]{:S(2)}, u32[]{:S(2)}) %collective-permute-start.17) | collective-permute-done | bytes 1081376 | tf_op jit(solution)/shard_map/ppermute | solution.py:287
  167.7 8.5 %collective-permute-done.18.refs_2_ = bf16[4,264,512]{2,1,0:T(8,128)(2,1)} collective-permute-done((bf16[4,264,512]{2,1,0:T(8,128)(2,1)}, bf16[4,264,512]{2,1,0:T(8,128)(2,1)}, u32[]{:S(2)}, u32[]{:S(2)}) %collective-permute-start.18) | collective-permute-done | bytes 1081376 | tf_op jit(solution)/shard_map/ppermute | solution.py:287
  176.2 7.2 %products.6 = f32[4,192,512]{2,1,0:T(8,128)} custom-call(s32[9]{0:T(128)} %get-tuple-element.166.table_ref, bf16[8,4,192,264]{3,2,1,0:T(8,128)(2,1)} %arranged.3.rows_ref, f32[4,264,2048]{2,1,0:T(8,128)} %refs_2_.15, bf16[4,264,512]{2,1,0:T(8,128)(2,1)} %copy-done.10, bf16[4,264,512]{2,1,0:T(8,128)(2,1)} %collective-permute-done.14.refs_1_, ...), custom_call_target="tpu_custom_call" | custom-call | flops 1 | bytes 1 | tf_op jit(solution)/shard_map/products/pallas_call | solution.py:156
  183.4 6.1 %collective-permute-done.16 = f32[4,192,512]{2,1,0:T(8,128)S(1)} collective-permute-done((f32[4,192,512]{2,1,0:T(8,128)}, f32[4,192,512]{2,1,0:T(8,128)S(1)}, u32[]{:S(2)}, u32[]{:S(2)}) %collective-permute-start.16) | collective-permute-done | bytes 1572896 | tf_op jit(solution)/shard_map/ppermute | solution.py:292
  189.5 1.7 slice.26
  192.1 7.0 %psum.14 = f32[4,192]{1,0:T(4,128)S(1)} all-reduce(f32[4,192]{1,0:T(4,128)S(1)} %multiply_reduce_fusion.1), channel_id=1, replica_groups=mesh['path'=8,'shard'=4] {'shard'}, use_global_device_ids=true, to_apply=%region_8.10 | all-reduce | flops 768 | bytes 6144 | tf_op jit(solution)/shard_map/psum | solution.py:369
  199.1 1.7 collective-permute-start.19
  200.8 7.9 %collective-permute-done.19 = f32[4,192]{1,0:T(4,128)S(1)} collective-permute-done((f32[4,192]{1,0:T(4,128)S(1)}, f32[4,192]{1,0:T(4,128)S(1)}, u32[]{:S(2)}, u32[]{:S(2)}) %collective-permute-start.19) | collective-permute-done | bytes 3104 | tf_op jit(solution)/shard_map/ppermute | solution.py:287
  208.7 1.5 collective-permute-start.20
  210.3 2.1 collective-permute-done.20
  212.4 2.5 broadcast_divide_fusion
  214.8 12.4 %collective-permute-done.21 = f32[2,192,512]{2,1,0:T(8,128)S(1)} collective-permute-done((f32[2,192,512]{2,1,0:T(8,128)S(1)}, f32[2,192,512]{2,1,0:T(8,128)S(1)}, u32[]{:S(2)}, u32[]{:S(2)}) %collective-permute-start.21) | collective-permute-done | bytes 786464 | tf_op jit(solution)/shard_map/ppermute | solution.py:292
  227.4 1.6 collective-permute-start.24
  229.0 3.0 collective-permute-start.22
  232.0 7.3 %products.7 = f32[4,192,512]{2,1,0:T(8,128)} custom-call(s32[9]{0:T(128)} %get-tuple-element.164.table_ref, bf16[8,4,192,264]{3,2,1,0:T(8,128)(2,1)} %arranged.3.rows_ref, f32[4,264,2048]{2,1,0:T(8,128)} %refs_2_.15, bf16[4,264,512]{2,1,0:T(8,128)(2,1)} %copy-done.10, bf16[4,264,512]{2,1,0:T(8,128)(2,1)} %collective-permute-done.14.refs_1_, ...), custom_call_target="tpu_custom_call" | custom-call | flops 1 | bytes 1 | tf_op jit(solution)/shard_map/products/pallas_call | solution.py:156
  239.3 7.6 %collective-permute-done.24.refs_0_ = bf16[4,192,512]{2,1,0:T(8,128)(2,1)S(1)} collective-permute-done((bf16[4,192,512]{2,1,0:T(8,128)(2,1)S(1)}, bf16[4,192,512]{2,1,0:T(8,128)(2,1)S(1)}, u32[]{:S(2)}, u32[]{:S(2)}) %collective-permute-start.24) | collective-permute-done | bytes 786464 | tf_op jit(solution)/shard_map/ppermute | solution.py:287
  246.9 18.0 %collective-permute-done.23.refs_0_ = bf16[4,192,512]{2,1,0:T(8,128)(2,1)} collective-permute-done((bf16[4,192,512]{2,1,0:T(8,128)(2,1)S(1)}, bf16[4,192,512]{2,1,0:T(8,128)(2,1)}, u32[]{:S(2)}, u32[]{:S(2)}) %collective-permute-start.23) | collective-permute-done | bytes 786464 | tf_op jit(solution)/shard_map/ppermute | solution.py:287
  266.7 1.5 collective-permute-start.26
  269.5 2.6 collective-permute-start.28
  273.9 2.4 constant_dynamic-slice_fusion.1
  276.3 2.4 copy.32
  278.7 2.4 constant_dynamic-slice_fusion
  281.2 2.4 copy.33
  283.6 7.6 %updated.8 = (f32[4,264,2048]{2,1,0:T(8,128)}, bf16[4,264,2048]{2,1,0:T(8,128)(2,1)}) custom-call(s32[11]{0:T(128)} %get-tuple-element.161.table_ref, bf16[8,264,192]{2,1,0:T(8,128)(2,1)} %bitcast.46, bf16[4,192,512]{2,1,0:T(8,128)(2,1)} %copy-done.14, bf16[4,192,512]{2,1,0:T(8,128)(2,1)} %collective-permute-done.22.refs_1_, f32[4,264,2048]{2,1,0:T(8,128)} %refs_2_.15, ...), custom_call_target="tpu_custom_call" | custom-call | flops 1 | bytes 1 | tf_op jit(solution)/shard_map/updated/pallas_call | solution.py:235
  291.2 9.3 %collective-permute-done.26.refs_1_ = bf16[4,192,512]{2,1,0:T(8,128)(2,1)} collective-permute-done((bf16[4,192,512]{2,1,0:T(8,128)(2,1)}, bf16[4,192,512]{2,1,0:T(8,128)(2,1)}, u32[]{:S(2)}, u32[]{:S(2)}) %collective-permute-start.26) | collective-permute-done | bytes 786464 | tf_op jit(solution)/shard_map/ppermute | solution.py:287
  300.6 4.6 %collective-permute-done.28 = f32[2,192,512]{2,1,0:T(8,128)S(1)} collective-permute-done((f32[2,192,512]{2,1,0:T(8,128)}, f32[2,192,512]{2,1,0:T(8,128)S(1)}, u32[]{:S(2)}, u32[]{:S(2)}) %collective-permute-start.28) | collective-permute-done | bytes 786464 | tf_op jit(solution)/shard_map/ppermute | solution.py:292
  306.1 5.6 %psum.15 = f32[4,192]{1,0:T(4,128)S(1)} all-reduce(f32[4,192]{1,0:T(4,128)S(1)} %multiply_reduce_fusion), channel_id=1, replica_groups=mesh['path'=8,'shard'=4] {'shard'}, use_global_device_ids=true, to_apply=%region_10.12 | all-reduce | flops 768 | bytes 6144 | tf_op jit(solution)/shard_map/psum | solution.py:369
  311.8 3.6 collective-permute-done.29
  317.4 1.7 collective-permute-done.30
  319.1 3.2 fusion.6.refs_0_
  322.9 7.4 %updated.9 = (f32[4,264,2048]{2,1,0:T(8,128)}, bf16[4,264,2048]{2,1,0:T(8,128)(2,1)}) custom-call(s32[11]{0:T(128)} %get-tuple-element.158.table_ref, bf16[8,264,192]{2,1,0:T(8,128)(2,1)} %bitcast.47, bf16[4,192,512]{2,1,0:T(8,128)(2,1)} %collective-permute-done.23.refs_0_, ...), custom_call_target="tpu_custom_call", output_to_operand_aliasing={{0}: (6, {}), {1}: (7, {})} | custom-call | flops 1 | bytes 1 | tf_op jit(solution)/shard_map/updated/pallas_call | solution.py:235
  330.3 2.7 collective-permute-start.31
  333.0 3.6 collective-permute-done.32.refs_1_
  336.6 14.3 %collective-permute-done.34.refs_0_ = bf16[4,192,512]{2,1,0:T(8,128)(2,1)S(1)} collective-permute-done((bf16[4,192,512]{2,1,0:T(8,128)(2,1)S(1)}, bf16[4,192,512]{2,1,0:T(8,128)(2,1)S(1)}, u32[]{:S(2)}, u32[]{:S(2)}) %collective-permute-start.34) | collective-permute-done | bytes 786464 | tf_op jit(solution)/shard_map/ppermute | solution.py:287
  350.9 1.6 collective-permute-start.35
  352.5 7.4 %updated.10 = (f32[4,264,2048]{2,1,0:T(8,128)}, bf16[4,264,2048]{2,1,0:T(8,128)(2,1)}) custom-call(s32[11]{0:T(128)} %get-tuple-element.157.table_ref, bf16[8,264,192]{2,1,0:T(8,128)(2,1)} %bitcast.48, bf16[4,192,512]{2,1,0:T(8,128)(2,1)} %copy-done.16, ...), custom_call_target="tpu_custom_call", output_to_operand_aliasing={{0}: (6, {}), {1}: (7, {})} | custom-call | flops 1 | bytes 1 | tf_op jit(solution)/shard_map/updated/pallas_call | solution.py:235
  359.9 7.5 %updated.11 = (f32[4,264,2048]{2,1,0:T(8,128)}, bf16[4,264,2048]{2,1,0:T(8,128)(2,1)}) custom-call(s32[11]{0:T(128)} %get-tuple-element.159.table_ref, bf16[8,264,192]{2,1,0:T(8,128)(2,1)} %bitcast.49, bf16[4,192,512]{2,1,0:T(8,128)(2,1)} %collective-permute-done.27.refs_0_, ...), custom_call_target="tpu_custom_call", output_to_operand_aliasing={{0}: (6, {}), {1}: (7, {})} | custom-call | flops 1 | bytes 1 | tf_op jit(solution)/shard_map/updated/pallas_call | solution.py:235
  368.5 1.7 collective-permute-start.36
  370.5 7.5 %updated.12 = (f32[4,264,2048]{2,1,0:T(8,128)}, bf16[4,264,2048]{2,1,0:T(8,128)(2,1)}) custom-call(s32[11]{0:T(128)} %get-tuple-element.162.table_ref, bf16[8,264,192]{2,1,0:T(8,128)(2,1)} %bitcast.42, bf16[4,192,512]{2,1,0:T(8,128)(2,1)} %copy-done.13, bf16[4,192,512]{2,1,0:T(8,128)(2,1)} %copy-done.20, f32[4,264,2048]{2,1,0:T(8,128)} %refs_2_.19, ...), custom_call_target="tpu_custom_call" | custom-call | flops 1 | bytes 1 | tf_op jit(solution)/shard_map/updated/pallas_call | solution.py:235
  377.9 6.9 %collective-permute-done.36.refs_1_ = bf16[4,192,512]{2,1,0:T(8,128)(2,1)S(1)} collective-permute-done((bf16[4,192,512]{2,1,0:T(8,128)(2,1)S(1)}, bf16[4,192,512]{2,1,0:T(8,128)(2,1)S(1)}, u32[]{:S(2)}, u32[]{:S(2)}) %collective-permute-start.36) | collective-permute-done | bytes 786464 | tf_op jit(solution)/shard_map/ppermute | solution.py:287
  388.0 7.5 %updated.13 = (f32[4,264,2048]{2,1,0:T(8,128)}, bf16[4,264,2048]{2,1,0:T(8,128)(2,1)}) custom-call(s32[11]{0:T(128)} %get-tuple-element.143.table_ref, bf16[8,264,192]{2,1,0:T(8,128)(2,1)} %bitcast.43, bf16[4,192,512]{2,1,0:T(8,128)(2,1)} %copy-done.18, bf16[4,192,512]{2,1,0:T(8,128)(2,1)} %copy-done.24, ...), custom_call_target="tpu_custom_call", output_to_operand_aliasing={{0}: (6, {}), {1}: (7, {})} | custom-call | flops 1 | bytes 1 | tf_op jit(solution)/shard_map/updated/pallas_call | solution.py:235
  395.5 7.5 %updated.14 = (f32[4,264,2048]{2,1,0:T(8,128)}, bf16[4,264,2048]{2,1,0:T(8,128)(2,1)}) custom-call(s32[11]{0:T(128)} %get-tuple-element.145.table_ref, bf16[8,264,192]{2,1,0:T(8,128)(2,1)} %bitcast.44, bf16[4,192,512]{2,1,0:T(8,128)(2,1)} %copy-done.17, bf16[4,192,512]{2,1,0:T(8,128)(2,1)} %copy-done.22, ...), custom_call_target="tpu_custom_call", output_to_operand_aliasing={{0}: (6, {}), {1}: (7, {})} | custom-call | flops 1 | bytes 1 | tf_op jit(solution)/shard_map/updated/pallas_call | solution.py:235
  403.8 7.6 %updated.15 = (f32[4,264,2048]{2,1,0:T(8,128)}, bf16[4,264,2048]{2,1,0:T(8,128)(2,1)}) custom-call(s32[11]{0:T(128)} %pad_add_fusion.10.table_ref, bf16[8,264,192]{2,1,0:T(8,128)(2,1)} %bitcast.45, bf16[4,192,512]{2,1,0:T(8,128)(2,1)} %copy-done.19, bf16[4,192,512]{2,1,0:T(8,128)(2,1)} %copy-done.23, ...), custom_call_target="tpu_custom_call", output_to_operand_aliasing={{0}: (6, {}), {1}: (7, {})} | custom-call | flops 1 | bytes 1 | tf_op jit(solution)/shard_map/updated/pallas_call | solution.py:235
  (151 shorter events, 37.1 us)
Async XLA Ops:
  0.6 13.2 %copy-start = (bf16[192,2112]{1,0:T(8,128)(2,1)S(1)}, bf16[192,2112]{1,0:T(8,128)(2,1)}, u32[]{:S(2)}) copy-start(bf16[192,2112]{1,0:T(8,128)(2,1)} %param.11) | copy-start | bytes 2433028
  0.7 9.6 %copy-start.27 = (s32[1,24]{1,0:T(1,128)S(1)}, s32[1,24]{1,0:T(1,128)}, u32[]{:S(2)}) copy-start(s32[1,24]{1,0:T(1,128)} %param.13) | copy-start | bytes 292
  0.7 9.9 %copy-start.28 = (s32[1,24]{1,0:T(1,128)S(1)}, s32[1,24]{1,0:T(1,128)}, u32[]{:S(2)}) copy-start(s32[1,24]{1,0:T(1,128)} %param.14) | copy-start | bytes 292
  5.7 46.6 %collective-permute-start.4 = (bf16[4,264,512]{2,1,0:T(8,128)(2,1)}, bf16[4,264,512]{2,1,0:T(8,128)(2,1)S(1)}, u32[]{:S(2)}, u32[]{:S(2)}) collective-permute-start(bf16[4,264,512]{2,1,0:T(8,128)(2,1)} %get-tuple-element.74), channel_id=1, source_target_pairs={{0,4},{4,0},{8,12},{12,8},{16,20},{20,16},{24,28},{28,24},{1,5},{5... | collective-permute-start | bytes 3244040 | tf_op jit(solution)/shard_map/ppermute | solution.py:287
  8.7 43.7 %collective-permute-start.5 = (bf16[4,264,512]{2,1,0:T(8,128)(2,1)}, bf16[4,264,512]{2,1,0:T(8,128)(2,1)S(1)}, u32[]{:S(2)}, u32[]{:S(2)}) collective-permute-start(bf16[4,264,512]{2,1,0:T(8,128)(2,1)} %get-tuple-element.75), channel_id=1, source_target_pairs={{0,8},{4,12},{8,0},{12,4},{16,24},{20,28},{24,16},{28,20},{1,9},{5... | collective-permute-start | bytes 3244040 | tf_op jit(solution)/shard_map/ppermute | solution.py:287
  14.3 41.7 %copy-start.26 = (s32[8,2]{0,1:T(2,128)S(1)}, s32[8,2]{0,1:T(2,128)}, u32[]{:S(2)}) copy-start(s32[8,2]{0,1:T(2,128)} %param.15) | copy-start | bytes 196
  15.6 22.4 %collective-permute-start = (bf16[2,2,24,1056]{3,2,1,0:T(8,128)(2,1)S(1)}, bf16[2,2,24,1056]{3,2,1,0:T(8,128)(2,1)S(1)}, u32[]{:S(2)}, u32[]{:S(2)}) collective-permute-start(bf16[2,2,24,1056]{3,2,1,0:T(8,128)(2,1)S(1)} %get-tuple-element.154), channel_id=1, source_target_pairs={{0,16},{4,20},{8,24},{12,28},{16,0},{20,4},{24,8},{28,12},{1,17},{... | collective-permute-start | bytes 608264 | tf_op jit(solution)/shard_map/ppermute | solution.py:292
  38.1 10.9 %collective-permute-start.2 = (bf16[2,2,2,24,1056]{4,3,2,1,0:T(8,128)(2,1)S(1)}, bf16[2,2,2,24,1056]{4,3,2,1,0:T(8,128)(2,1)}, u32[]{:S(2)}, u32[]{:S(2)}) collective-permute-start(bf16[2,2,2,24,1056]{4,3,2,1,0:T(8,128)(2,1)S(1)} %get-tuple-element.152), channel_id=1, source_target_pairs={{0,4},{4,0},{8,12},{12,8},{16,20},{20,16},{24,28},{28,24},{1,5},{5... | collective-permute-start | bytes 1216520 | tf_op jit(solution)/shard_map/ppermute | solution.py:287
  38.7 12.3 %collective-permute-start.1 = (bf16[2,2,2,24,1056]{4,3,2,1,0:T(8,128)(2,1)S(1)}, bf16[2,2,2,24,1056]{4,3,2,1,0:T(8,128)(2,1)}, u32[]{:S(2)}, u32[]{:S(2)}) collective-permute-start(bf16[2,2,2,24,1056]{4,3,2,1,0:T(8,128)(2,1)S(1)} %get-tuple-element.152), channel_id=1, source_target_pairs={{0,8},{4,12},{8,0},{12,4},{16,24},{20,28},{24,16},{28,20},{1,9},{5... | collective-permute-start | bytes 1216520 | tf_op jit(solution)/shard_map/ppermute | solution.py:287
  42.2 10.2 %collective-permute-start.3 = (bf16[2,2,2,24,1056]{4,3,2,1,0:T(8,128)(2,1)S(1)}, bf16[2,2,2,24,1056]{4,3,2,1,0:T(8,128)(2,1)S(1)}, u32[]{:S(2)}, u32[]{:S(2)}) collective-permute-start(bf16[2,2,2,24,1056]{4,3,2,1,0:T(8,128)(2,1)S(1)} %get-tuple-element.152), channel_id=1, source_target_pairs={{0,2},{1,3},{2,0},{3,1},{4,6},{5,7},{6,4},{7,5},{8,10},{9,11},{10,... | collective-permute-start | bytes 1216520 | tf_op jit(solution)/shard_map/ppermute | solution.py:297
  52.3 3.6 copy-start.25
  52.3 10.1 %copy-start.8 = (bf16[4,264,512]{2,1,0:T(8,128)(2,1)}, bf16[4,264,512]{2,1,0:T(8,128)(2,1)S(1)}, u32[]{:S(2)}) copy-start(bf16[4,264,512]{2,1,0:T(8,128)(2,1)S(1)} %collective-permute-done.4.refs_0_) | copy-start | bytes 3244036
  52.4 3.6 copy-start.9
  52.4 19.9 %collective-permute-start.7 = (bf16[2,2,2,24,1056]{4,3,2,1,0:T(8,128)(2,1)}, bf16[2,2,2,24,1056]{4,3,2,1,0:T(8,128)(2,1)}, u32[]{:S(2)}, u32[]{:S(2)}) collective-permute-start(bf16[2,2,2,24,1056]{4,3,2,1,0:T(8,128)(2,1)} %collective-permute-done.1), channel_id=1, source_target_pairs={{0,2},{1,3},{2,0},{3,1},{4,6},{5,7},{6,4},{7,5},{8,10},{9,11},{10,... | collective-permute-start | bytes 1216520 | tf_op jit(solution)/shard_map/ppermute | solution.py:297
  53.9 18.3 %collective-permute-start.6 = (bf16[2,2,2,24,1056]{4,3,2,1,0:T(8,128)(2,1)}, bf16[2,2,2,24,1056]{4,3,2,1,0:T(8,128)(2,1)}, u32[]{:S(2)}, u32[]{:S(2)}) collective-permute-start(bf16[2,2,2,24,1056]{4,3,2,1,0:T(8,128)(2,1)} %collective-permute-done.1), channel_id=1, source_target_pairs={{0,4},{4,0},{8,12},{12,8},{16,20},{20,16},{24,28},{28,24},{1,5},{5... | collective-permute-start | bytes 1216520 | tf_op jit(solution)/shard_map/ppermute | solution.py:287
  55.4 16.8 %collective-permute-start.8 = (bf16[2,2,2,24,1056]{4,3,2,1,0:T(8,128)(2,1)}, bf16[2,2,2,24,1056]{4,3,2,1,0:T(8,128)(2,1)}, u32[]{:S(2)}, u32[]{:S(2)}) collective-permute-start(bf16[2,2,2,24,1056]{4,3,2,1,0:T(8,128)(2,1)} %collective-permute-done.2), channel_id=1, source_target_pairs={{0,2},{1,3},{2,0},{3,1},{4,6},{5,7},{6,4},{7,5},{8,10},{9,11},{10,... | collective-permute-start | bytes 1216520 | tf_op jit(solution)/shard_map/ppermute | solution.py:297
  57.1 5.3 %copy-start.5 = (bf16[2,2,2,2,24,1056]{5,4,3,2,1,0:T(8,128)(2,1)}, bf16[2,2,2,2,24,1056]{5,4,3,2,1,0:T(8,128)(2,1)S(1)}, u32[]{:S(2)}) copy-start(bf16[2,2,2,2,24,1056]{5,4,3,2,1,0:T(8,128)(2,1)S(1)} %pad_maximum_fusion.refs_0_) | copy-start | bytes 2433028
  57.1 26.5 %collective-permute-start.10 = (bf16[2,2,2,2,24,1056]{5,4,3,2,1,0:T(8,128)(2,1)S(1)}, bf16[2,2,2,2,24,1056]{5,4,3,2,1,0:T(8,128)(2,1)S(1)}, u32[]{:S(2)}, u32[]{:S(2)}) collective-permute-start(bf16[2,2,2,2,24,1056]{5,4,3,2,1,0:T(8,128)(2,1)S(1)} %pad_maximum_fusion.refs_0_), channel_id=1, source_target_pairs={{0,1},{1,0},{2,3},{3,2},{4,5},{5,4},{6,7},{7,6},{8,9},{9,8},{10,11... | collective-permute-start | bytes 2433032 | tf_op jit(solution)/shard_map/ppermute | solution.py:297
  62.4 49.5 %collective-permute-start.15 = (bf16[4,264,512]{2,1,0:T(8,128)(2,1)}, bf16[4,264,512]{2,1,0:T(8,128)(2,1)}, u32[]{:S(2)}, u32[]{:S(2)}) collective-permute-start(bf16[4,264,512]{2,1,0:T(8,128)(2,1)} %get-tuple-element.90), channel_id=1, source_target_pairs={{0,12},{4,8},{8,4},{12,0},{16,28},{20,24},{24,20},{28,16},{1,13},{... | collective-permute-start | bytes 3244040 | tf_op jit(solution)/shard_map/ppermute | solution.py:287
  72.2 8.7 %collective-permute-start.9 = (bf16[2,2,2,24,1056]{4,3,2,1,0:T(8,128)(2,1)}, bf16[2,2,2,24,1056]{4,3,2,1,0:T(8,128)(2,1)S(1)}, u32[]{:S(2)}, u32[]{:S(2)}) collective-permute-start(bf16[2,2,2,24,1056]{4,3,2,1,0:T(8,128)(2,1)} %collective-permute-done.6), channel_id=1, source_target_pairs={{0,2},{1,3},{2,0},{3,1},{4,6},{5,7},{6,4},{7,5},{8,10},{9,11},{10,... | collective-permute-start | bytes 1216520 | tf_op jit(solution)/shard_map/ppermute | solution.py:297
  75.0 8.7 %copy-start.6 = (bf16[2,2,2,2,24,1056]{5,4,3,2,1,0:T(8,128)(2,1)}, bf16[2,2,2,2,24,1056]{5,4,3,2,1,0:T(8,128)(2,1)S(1)}, u32[]{:S(2)}) copy-start(bf16[2,2,2,2,24,1056]{5,4,3,2,1,0:T(8,128)(2,1)S(1)} %pad_maximum_fusion.2.refs_2_) | copy-start | bytes 2433028
  75.0 12.1 %collective-permute-start.12 = (bf16[2,2,2,2,24,1056]{5,4,3,2,1,0:T(8,128)(2,1)S(1)}, bf16[2,2,2,2,24,1056]{5,4,3,2,1,0:T(8,128)(2,1)}, u32[]{:S(2)}, u32[]{:S(2)}) collective-permute-start(bf16[2,2,2,2,24,1056]{5,4,3,2,1,0:T(8,128)(2,1)S(1)} %pad_maximum_fusion.2.refs_2_), channel_id=1, source_target_pairs={{0,1},{1,0},{2,3},{3,2},{4,5},{5,4},{6,7},{7,6},{8,9},{9,8},{10,11... | collective-permute-start | bytes 2433032 | tf_op jit(solution)/shard_map/ppermute | solution.py:297
  77.5 9.6 %collective-permute-start.11 = (bf16[2,2,2,2,24,1056]{5,4,3,2,1,0:T(8,128)(2,1)}, bf16[2,2,2,2,24,1056]{5,4,3,2,1,0:T(8,128)(2,1)}, u32[]{:S(2)}, u32[]{:S(2)}) collective-permute-start(bf16[2,2,2,2,24,1056]{5,4,3,2,1,0:T(8,128)(2,1)} %pad_maximum_fusion.1.refs_1_), channel_id=1, source_target_pairs={{0,1},{1,0},{2,3},{3,2},{4,5},{5,4},{6,7},{7,6},{8,9},{9,8},{10,11... | collective-permute-start | bytes 2433032 | tf_op jit(solution)/shard_map/ppermute | solution.py:297
  80.9 31.0 %collective-permute-start.14 = (bf16[4,264,512]{2,1,0:T(8,128)(2,1)}, bf16[4,264,512]{2,1,0:T(8,128)(2,1)}, u32[]{:S(2)}, u32[]{:S(2)}) collective-permute-start(bf16[4,264,512]{2,1,0:T(8,128)(2,1)} %get-tuple-element.86), channel_id=1, source_target_pairs={{0,8},{4,12},{8,0},{12,4},{16,24},{20,28},{24,16},{28,20},{1,9},{5... | collective-permute-start | bytes 3244040 | tf_op jit(solution)/shard_map/ppermute | solution.py:287
  84.6 2.6 collective-permute-start.13
  87.2 0.9 copy-start.12
  119.1 70.4 %collective-permute-start.16 = (f32[4,192,512]{2,1,0:T(8,128)}, f32[4,192,512]{2,1,0:T(8,128)S(1)}, u32[]{:S(2)}, u32[]{:S(2)}) collective-permute-start(f32[4,192,512]{2,1,0:T(8,128)} %products.5), channel_id=1, source_target_pairs={{0,16},{4,20},{8,24},{12,28},{16,0},{20,4},{24,8},{28,12},{1,17},{... | collective-permute-start | bytes 4718600 | tf_op jit(solution)/shard_map/ppermute | solution.py:292
  119.4 48.3 %collective-permute-start.17 = (bf16[4,264,512]{2,1,0:T(8,128)(2,1)}, bf16[4,264,512]{2,1,0:T(8,128)(2,1)S(1)}, u32[]{:S(2)}, u32[]{:S(2)}) collective-permute-start(bf16[4,264,512]{2,1,0:T(8,128)(2,1)} %get-tuple-element.93), channel_id=1, source_target_pairs={{0,4},{4,0},{8,12},{12,8},{16,20},{20,16},{24,28},{28,24},{1,5},{5... | collective-permute-start | bytes 3244040 | tf_op jit(solution)/shard_map/ppermute | solution.py:287
  120.9 55.3 %collective-permute-start.18 = (bf16[4,264,512]{2,1,0:T(8,128)(2,1)}, bf16[4,264,512]{2,1,0:T(8,128)(2,1)}, u32[]{:S(2)}, u32[]{:S(2)}) collective-permute-start(bf16[4,264,512]{2,1,0:T(8,128)(2,1)} %get-tuple-element.95), channel_id=1, source_target_pairs={{0,12},{4,8},{8,4},{12,0},{16,28},{20,24},{24,20},{28,16},{1,13},{... | collective-permute-start | bytes 3244040 | tf_op jit(solution)/shard_map/ppermute | solution.py:287
  167.7 8.5 %copy-start.10 = (bf16[4,264,512]{2,1,0:T(8,128)(2,1)}, bf16[4,264,512]{2,1,0:T(8,128)(2,1)S(1)}, u32[]{:S(2)}) copy-start(bf16[4,264,512]{2,1,0:T(8,128)(2,1)S(1)} %collective-permute-done.17.refs_0_) | copy-start | bytes 3244036
  183.4 7.9 %copy-start.2 = (f32[4,192,512]{2,1,0:T(8,128)S(1)}, f32[4,192,512]{2,1,0:T(8,128)}, u32[]{:S(2)}) copy-start(f32[4,192,512]{2,1,0:T(8,128)} %products.4) | copy-start | bytes 4718596
  189.5 2.6 copy-start.3
  191.3 36.0 %collective-permute-start.21 = (f32[2,192,512]{2,1,0:T(8,128)S(1)}, f32[2,192,512]{2,1,0:T(8,128)S(1)}, u32[]{:S(2)}, u32[]{:S(2)}) collective-permute-start(f32[2,192,512]{2,1,0:T(8,128)S(1)} %slice.26), channel_id=1, source_target_pairs={{0,16},{4,20},{8,24},{12,28},{16,0},{20,4},{24,8},{28,12},{1,17},{... | collective-permute-start | bytes 2359304 | tf_op jit(solution)/shard_map/ppermute | solution.py:292
  199.1 9.6 %collective-permute-start.19 = (f32[4,192]{1,0:T(4,128)S(1)}, f32[4,192]{1,0:T(4,128)S(1)}, u32[]{:S(2)}, u32[]{:S(2)}) collective-permute-start(f32[4,192]{1,0:T(4,128)S(1)} %psum.14), channel_id=1, source_target_pairs={{0,8},{4,12},{8,0},{12,4},{16,24},{20,28},{24,16},{28,20},{1,9},{5... | collective-permute-start | bytes 9224 | tf_op jit(solution)/shard_map/ppermute | solution.py:287
  208.7 3.6 collective-permute-start.20
  227.4 11.9 %copy-start.14 = (bf16[4,192,512]{2,1,0:T(8,128)(2,1)}, bf16[4,192,512]{2,1,0:T(8,128)(2,1)S(1)}, u32[]{:S(2)}) copy-start(bf16[4,192,512]{2,1,0:T(8,128)(2,1)S(1)} %convert_element_type.21.refs_0_) | copy-start | bytes 2359300
  227.4 19.5 %collective-permute-start.24 = (bf16[4,192,512]{2,1,0:T(8,128)(2,1)S(1)}, bf16[4,192,512]{2,1,0:T(8,128)(2,1)S(1)}, u32[]{:S(2)}, u32[]{:S(2)}) collective-permute-start(bf16[4,192,512]{2,1,0:T(8,128)(2,1)S(1)} %convert_element_type.21.refs_0_), channel_id=1, source_target_pairs={{0,4},{4,0},{8,12},{12,8},{16,20},{20,16},{24,28},{28,24},{1,5},{5... | collective-permute-start | bytes 2359304 | tf_op jit(solution)/shard_map/ppermute | solution.py:287
  229.0 35.9 %collective-permute-start.23 = (bf16[4,192,512]{2,1,0:T(8,128)(2,1)S(1)}, bf16[4,192,512]{2,1,0:T(8,128)(2,1)}, u32[]{:S(2)}, u32[]{:S(2)}) collective-permute-start(bf16[4,192,512]{2,1,0:T(8,128)(2,1)S(1)} %convert_element_type.21.refs_0_), channel_id=1, source_target_pairs={{0,8},{4,12},{8,0},{12,4},{16,24},{20,28},{24,16},{28,20},{1,9},{5... | collective-permute-start | bytes 2359304 | tf_op jit(solution)/shard_map/ppermute | solution.py:287
  229.0 37.2 %collective-permute-start.22 = (bf16[4,192,512]{2,1,0:T(8,128)(2,1)S(1)}, bf16[4,192,512]{2,1,0:T(8,128)(2,1)}, u32[]{:S(2)}, u32[]{:S(2)}) collective-permute-start(bf16[4,192,512]{2,1,0:T(8,128)(2,1)S(1)} %convert_element_type.21.refs_0_), channel_id=1, source_target_pairs={{0,16},{4,20},{8,24},{12,28},{16,0},{20,4},{24,8},{28,12},{1,17},{... | collective-permute-start | bytes 2359304 | tf_op jit(solution)/shard_map/ppermute | solution.py:292
  232.0 36.5 %copy-start.7 = (f32[4,192,512]{2,1,0:T(8,128)S(1)}, f32[4,192,512]{2,1,0:T(8,128)}, u32[]{:S(2)}) copy-start(f32[4,192,512]{2,1,0:T(8,128)} %products.6) | copy-start | bytes 4718596
  246.9 22.6 %copy-start.16 = (bf16[4,192,512]{2,1,0:T(8,128)(2,1)}, bf16[4,192,512]{2,1,0:T(8,128)(2,1)S(1)}, u32[]{:S(2)}) copy-start(bf16[4,192,512]{2,1,0:T(8,128)(2,1)S(1)} %collective-permute-done.24.refs_0_) | copy-start | bytes 2359300
  266.2 25.0 %collective-permute-start.27 = (bf16[4,192,512]{2,1,0:T(8,128)(2,1)}, bf16[4,192,512]{2,1,0:T(8,128)(2,1)}, u32[]{:S(2)}, u32[]{:S(2)}) collective-permute-start(bf16[4,192,512]{2,1,0:T(8,128)(2,1)} %collective-permute-done.23.refs_0_), channel_id=1, source_target_pairs={{0,4},{4,0},{8,12},{12,8},{16,20},{20,16},{24,28},{28,24},{1,5},{5... | collective-permute-start | bytes 2359304 | tf_op jit(solution)/shard_map/ppermute | solution.py:287
  266.7 33.8 %collective-permute-start.26 = (bf16[4,192,512]{2,1,0:T(8,128)(2,1)}, bf16[4,192,512]{2,1,0:T(8,128)(2,1)}, u32[]{:S(2)}, u32[]{:S(2)}) collective-permute-start(bf16[4,192,512]{2,1,0:T(8,128)(2,1)} %collective-permute-done.22.refs_1_), channel_id=1, source_target_pairs={{0,4},{4,0},{8,12},{12,8},{16,20},{20,16},{24,28},{28,24},{1,5},{5... | collective-permute-start | bytes 2359304 | tf_op jit(solution)/shard_map/ppermute | solution.py:287
  268.2 32.4 %collective-permute-start.25 = (bf16[4,192,512]{2,1,0:T(8,128)(2,1)}, bf16[4,192,512]{2,1,0:T(8,128)(2,1)}, u32[]{:S(2)}, u32[]{:S(2)}) collective-permute-start(bf16[4,192,512]{2,1,0:T(8,128)(2,1)} %collective-permute-done.22.refs_1_), channel_id=1, source_target_pairs={{0,8},{4,12},{8,0},{12,4},{16,24},{20,28},{24,16},{28,20},{1,9},{5... | collective-permute-start | bytes 2359304 | tf_op jit(solution)/shard_map/ppermute | solution.py:287
  269.5 35.7 %collective-permute-start.28 = (f32[2,192,512]{2,1,0:T(8,128)}, f32[2,192,512]{2,1,0:T(8,128)S(1)}, u32[]{:S(2)}, u32[]{:S(2)}) collective-permute-start(f32[2,192,512]{2,1,0:T(8,128)} %slice.27), channel_id=1, source_target_pairs={{0,16},{4,20},{8,24},{12,28},{16,0},{20,4},{24,8},{28,12},{1,17},{... | collective-permute-start | bytes 2359304 | tf_op jit(solution)/shard_map/ppermute | solution.py:292
  283.6 21.6 %copy-start.4 = (f32[4,192,512]{2,1,0:T(8,128)S(1)}, f32[4,192,512]{2,1,0:T(8,128)}, u32[]{:S(2)}) copy-start(f32[4,192,512]{2,1,0:T(8,128)} %products.7) | copy-start | bytes 4718596
  311.7 3.7 collective-permute-start.29
  315.4 3.7 collective-permute-start.30
  315.9 20.7 %collective-permute-start.32 = (bf16[4,192,512]{2,1,0:T(8,128)(2,1)}, bf16[4,192,512]{2,1,0:T(8,128)(2,1)S(1)}, u32[]{:S(2)}, u32[]{:S(2)}) collective-permute-start(bf16[4,192,512]{2,1,0:T(8,128)(2,1)} %collective-permute-done.25.refs_1_), channel_id=1, source_target_pairs={{0,4},{4,0},{8,12},{12,8},{16,20},{20,16},{24,28},{28,24},{1,5},{5... | collective-permute-start | bytes 2359304 | tf_op jit(solution)/shard_map/ppermute | solution.py:287
  322.4 7.9 %copy-start.13 = (bf16[4,192,512]{2,1,0:T(8,128)(2,1)}, bf16[4,192,512]{2,1,0:T(8,128)(2,1)S(1)}, u32[]{:S(2)}) copy-start(bf16[4,192,512]{2,1,0:T(8,128)(2,1)S(1)} %fusion.6.refs_0_) | copy-start | bytes 2359300
  322.4 28.5 %collective-permute-start.34 = (bf16[4,192,512]{2,1,0:T(8,128)(2,1)S(1)}, bf16[4,192,512]{2,1,0:T(8,128)(2,1)S(1)}, u32[]{:S(2)}, u32[]{:S(2)}) collective-permute-start(bf16[4,192,512]{2,1,0:T(8,128)(2,1)S(1)} %fusion.6.refs_0_), channel_id=1, source_target_pairs={{0,4},{4,0},{8,12},{12,8},{16,20},{20,16},{24,28},{28,24},{1,5},{5... | collective-permute-start | bytes 2359304 | tf_op jit(solution)/shard_map/ppermute | solution.py:287
  322.8 28.0 %collective-permute-start.33 = (bf16[4,192,512]{2,1,0:T(8,128)(2,1)S(1)}, bf16[4,192,512]{2,1,0:T(8,128)(2,1)S(1)}, u32[]{:S(2)}, u32[]{:S(2)}) collective-permute-start(bf16[4,192,512]{2,1,0:T(8,128)(2,1)S(1)} %fusion.6.refs_0_), channel_id=1, source_target_pairs={{0,8},{4,12},{8,0},{12,4},{16,24},{20,28},{24,16},{28,20},{1,9},{5... | collective-permute-start | bytes 2359304 | tf_op jit(solution)/shard_map/ppermute | solution.py:287
  330.3 37.1 %collective-permute-start.31 = (bf16[4,192,512]{2,1,0:T(8,128)(2,1)S(1)}, bf16[4,192,512]{2,1,0:T(8,128)(2,1)S(1)}, u32[]{:S(2)}, u32[]{:S(2)}) collective-permute-start(bf16[4,192,512]{2,1,0:T(8,128)(2,1)S(1)} %fusion.6.refs_0_), channel_id=1, source_target_pairs={{0,16},{4,20},{8,24},{12,28},{16,0},{20,4},{24,8},{28,12},{1,17},{... | collective-permute-start | bytes 2359304 | tf_op jit(solution)/shard_map/ppermute | solution.py:292
  336.6 23.3 %copy-start.21 = (bf16[4,192,512]{2,1,0:T(8,128)(2,1)}, bf16[4,192,512]{2,1,0:T(8,128)(2,1)S(1)}, u32[]{:S(2)}) copy-start(bf16[4,192,512]{2,1,0:T(8,128)(2,1)S(1)} %collective-permute-done.32.refs_1_) | copy-start | bytes 2359300
  350.9 9.0 %copy-start.17 = (bf16[4,192,512]{2,1,0:T(8,128)(2,1)}, bf16[4,192,512]{2,1,0:T(8,128)(2,1)S(1)}, u32[]{:S(2)}) copy-start(bf16[4,192,512]{2,1,0:T(8,128)(2,1)S(1)} %collective-permute-done.34.refs_0_) | copy-start | bytes 2359300
  350.9 9.0 %copy-start.18 = (bf16[4,192,512]{2,1,0:T(8,128)(2,1)}, bf16[4,192,512]{2,1,0:T(8,128)(2,1)S(1)}, u32[]{:S(2)}) copy-start(bf16[4,192,512]{2,1,0:T(8,128)(2,1)S(1)} %collective-permute-done.33.refs_0_) | copy-start | bytes 2359300
  350.9 17.6 %collective-permute-start.35 = (bf16[4,192,512]{2,1,0:T(8,128)(2,1)S(1)}, bf16[4,192,512]{2,1,0:T(8,128)(2,1)S(1)}, u32[]{:S(2)}, u32[]{:S(2)}) collective-permute-start(bf16[4,192,512]{2,1,0:T(8,128)(2,1)S(1)} %collective-permute-done.33.refs_0_), channel_id=1, source_target_pairs={{0,4},{4,0},{8,12},{12,8},{16,20},{20,16},{24,28},{28,24},{1,5},{5... | collective-permute-start | bytes 2359304 | tf_op jit(solution)/shard_map/ppermute | solution.py:287
  367.4 3.1 copy-start.20
  368.5 9.5 %copy-start.19 = (bf16[4,192,512]{2,1,0:T(8,128)(2,1)}, bf16[4,192,512]{2,1,0:T(8,128)(2,1)S(1)}, u32[]{:S(2)}) copy-start(bf16[4,192,512]{2,1,0:T(8,128)(2,1)S(1)} %collective-permute-done.35.refs_0_) | copy-start | bytes 2359300
  368.5 16.3 %collective-permute-start.36 = (bf16[4,192,512]{2,1,0:T(8,128)(2,1)S(1)}, bf16[4,192,512]{2,1,0:T(8,128)(2,1)S(1)}, u32[]{:S(2)}, u32[]{:S(2)}) collective-permute-start(bf16[4,192,512]{2,1,0:T(8,128)(2,1)S(1)} %collective-permute-done.31.refs_1_), channel_id=1, source_target_pairs={{0,4},{4,0},{8,12},{12,8},{16,20},{20,16},{24,28},{28,24},{1,5},{5... | collective-permute-start | bytes 2359304 | tf_op jit(solution)/shard_map/ppermute | solution.py:287
  370.2 16.9 %collective-permute-start.38 = (bf16[4,192,512]{2,1,0:T(8,128)(2,1)S(1)}, bf16[4,192,512]{2,1,0:T(8,128)(2,1)S(1)}, u32[]{:S(2)}, u32[]{:S(2)}) collective-permute-start(bf16[4,192,512]{2,1,0:T(8,128)(2,1)S(1)} %collective-permute-done.31.refs_1_), channel_id=1, source_target_pairs={{0,8},{4,12},{8,0},{12,4},{16,24},{20,28},{24,16},{28,20},{1,9},{5... | collective-permute-start | bytes 2359304 | tf_op jit(solution)/shard_map/ppermute | solution.py:287
  384.8 10.7 %copy-start.22 = (bf16[4,192,512]{2,1,0:T(8,128)(2,1)}, bf16[4,192,512]{2,1,0:T(8,128)(2,1)S(1)}, u32[]{:S(2)}) copy-start(bf16[4,192,512]{2,1,0:T(8,128)(2,1)S(1)} %collective-permute-done.36.refs_1_) | copy-start | bytes 2359300
  384.8 18.1 %collective-permute-start.37 = (bf16[4,192,512]{2,1,0:T(8,128)(2,1)S(1)}, bf16[4,192,512]{2,1,0:T(8,128)(2,1)S(1)}, u32[]{:S(2)}, u32[]{:S(2)}) collective-permute-start(bf16[4,192,512]{2,1,0:T(8,128)(2,1)S(1)} %collective-permute-done.36.refs_1_), channel_id=1, source_target_pairs={{0,8},{4,12},{8,0},{12,4},{16,24},{20,28},{24,16},{28,20},{1,9},{5... | collective-permute-start | bytes 2359304 | tf_op jit(solution)/shard_map/ppermute | solution.py:287
  403.8 7.6 %copy-start.1 = (bf16[192,2112]{1,0:T(8,128)(2,1)S(1)}, bf16[192,2112]{1,0:T(8,128)(2,1)}, u32[]{:S(2)}) copy-start(bf16[192,2112]{1,0:T(8,128)(2,1)} %param.11) | copy-start | bytes 2433028
  (4 other events, 3.6 us)

commit v2 on v1

--- a/solution.py
+++ b/solution.py
@@ -396,9 +396,10 @@
         return [move(block, offset) for offset in others]
 
     normed_rows = arranged(0, place, team, path_count, mine, theirs)
-    normed_rows, down_near = tie(normed_rows, down_near)
     up_operands = (normed_rows, up_modules, up_master, [up_beside, up_near, up_across])
-    pre_moved = [move(part_of(offset, *up_operands), offset) for offset in others]
+    pre_parts = [part_of(offset, *up_operands) for offset in others]
+    pre_parts, down_near = tie(pre_parts, down_near)
+    pre_moved = [move(part, offset) for part, offset in zip(pre_parts, others)]
     pre_own = part_of(0, *up_operands)
     late_place, pre_own = tie(place, pre_own)
     grad_rows = arranged(1, late_place, team, path_count, mine, theirs)

time: 413 us -> 406 us (0.983)
  waiting for transfers between devices: 193 us -> 186 us
    ppermute x25, waiting for transfers between devices: 135 us -> 128 us  [trade(): lax.ppermute(value, 'path', [(i, i ^ mask) for i in range(path_count)])]
  transfers between devices with their start and end apart: 39 -> 39, of which waited for: 27 -> 27; matrix products, arithmetic and copies ran while one was open for 9% -> 9% of each run, Pallas kernels for 24% -> 26%
where the time goes in v2:
time: 406 us; the launch traced here: 404 us
  waiting for transfers between devices  186 us (46%)
  Pallas kernels  117 us (29%)
  starting transfers between devices  45 us (11%)
  other arithmetic  20.5 us (5%)
  local copies, waits for them, and re-layouts  19.5 us (5%)
  blocking collectives  12.7 us (3%)
    ppermute x25, waiting for transfers between devices, trade(): lax.ppermute(value, 'path', [(i, i ^ mask) for i in range(path_count)])  128 us
    pallas_call x8, Pallas kernels, updated(): pl.pallas_call(functools.partial(update_kernel, blocks, groups, tiles, le...  60 us
    ppermute x6, waiting for transfers between devices, move(): lax.ppermute(value, 'path', [(i, (i + team * offset) % path_count) for i...  44.2 us
    pallas_call x4, Pallas kernels, products(): pl.pallas_call(functools.partial(product_kernel, team, listed), out_shape...  28.8 us
    ppermute x25, starting transfers between devices, trade(): lax.ppermute(value, 'path', [(i, i ^ mask) for i in range(path_count)])  28.2 us
    pallas_call x2, Pallas kernels, arranged(): pl.pallas_call(functools.partial(arranged_kernel, team), out_shape=jax.Sh...  17.9 us
    ppermute x8, waiting for transfers between devices, share(): lax.ppermute(value, 'shard', [(i, i ^ mask) for i in range(shard_count)])  14.1 us
    psum x2, blocking collectives, row_sums(): summed = lax.psum(jnp.sum(values, axis=2), 'shard')  12.7 us
  transfers between devices with their start and end apart: 39, of which 27 were waited for; matrix products, arithmetic and copies ran while one was open for 9% of the time, Pallas kernels for 26%

profile of v2, /device:TPU:0, one launch (start us, length us, event | category | flops | bytes accessed | tf_op | source)
XLA Modules:
  0.0 404.3 jit_solution(15081361557844560600)
XLA Ops:
  0.7 5.0 %outgoing_weights.2 = (bf16[4,264,512]{2,1,0:T(8,128)(2,1)}, bf16[4,264,512]{2,1,0:T(8,128)(2,1)}, bf16[4,264,512]{2,1,0:T(8,128)(2,1)}) custom-call(s32[1]{0:T(128)} %bitcast.4.table_ref, f32[4,264,2048]{2,1,0:T(8,128)} %refs_2_.19, f32[4,264,2048]{2,1,0:T(8,128)} %refs_2_.19, f32[4,264,2048]{2,1,0:T(8,128)} %refs_2_.19), custom_call_target="tpu_custom_call" | custom-call | flops 1 | bytes 1 | tf_op jit(solution)/shard_map/outgoing_weights/pallas_call | solution.py:58
  5.7 3.0 collective-permute-start.4
  8.7 1.6 collective-permute-start.5
  11.7 2.2 convolution_convert_fusion
  15.6 2.7 collective-permute-start
  18.3 19.8 %collective-permute-done = bf16[2,2,24,1056]{3,2,1,0:T(8,128)(2,1)S(1)} collective-permute-done((bf16[2,2,24,1056]{3,2,1,0:T(8,128)(2,1)S(1)}, bf16[2,2,24,1056]{3,2,1,0:T(8,128)(2,1)S(1)}, u32[]{:S(2)}, u32[]{:S(2)}) %collective-permute-start) | collective-permute-done | bytes 202784 | tf_op jit(solution)/shard_map/ppermute | solution.py:292
  38.7 3.5 collective-permute-start.1
  43.7 5.3 %collective-permute-done.2 = bf16[2,2,2,24,1056]{4,3,2,1,0:T(8,128)(2,1)} collective-permute-done((bf16[2,2,2,24,1056]{4,3,2,1,0:T(8,128)(2,1)S(1)}, bf16[2,2,2,24,1056]{4,3,2,1,0:T(8,128)(2,1)}, u32[]{:S(2)}, u32[]{:S(2)}) %collective-permute-start.2) | collective-permute-done | bytes 405536 | tf_op jit(solution)/shard_map/ppermute | solution.py:287
  49.0 2.0 collective-permute-done.1
  52.4 1.6 collective-permute-start.7
  57.2 5.2 %outgoing_weights.3 = (bf16[4,264,512]{2,1,0:T(8,128)(2,1)}, bf16[4,264,512]{2,1,0:T(8,128)(2,1)}, bf16[4,264,512]{2,1,0:T(8,128)(2,1)}) custom-call(s32[1]{0:T(128)} %bitcast.4.table_ref, f32[4,264,2048]{2,1,0:T(8,128)} %refs_2_.15, f32[4,264,2048]{2,1,0:T(8,128)} %refs_2_.15, f32[4,264,2048]{2,1,0:T(8,128)} %refs_2_.15), custom_call_target="tpu_custom_call" | custom-call | flops 1 | bytes 1 | tf_op jit(solution)/shard_map/outgoing_weights/pallas_call | solution.py:58
  62.8 9.4 %collective-permute-done.8 = bf16[2,2,2,24,1056]{4,3,2,1,0:T(8,128)(2,1)} collective-permute-done((bf16[2,2,2,24,1056]{4,3,2,1,0:T(8,128)(2,1)}, bf16[2,2,2,24,1056]{4,3,2,1,0:T(8,128)(2,1)}, u32[]{:S(2)}, u32[]{:S(2)}) %collective-permute-start.8) | collective-permute-done | bytes 405536 | tf_op jit(solution)/shard_map/ppermute | solution.py:297
  75.1 2.4 pad_maximum_fusion.1.refs_1_
  77.7 3.2 collective-permute-done.9
  81.6 2.1 pad_maximum_fusion.3.refs_3_
  88.1 8.9 %arranged.2.rows_ref = bf16[8,4,192,264]{3,2,1,0:T(8,128)(2,1)} custom-call(s32[3]{0:T(128)} %pad_add_fusion.table_ref, bf16[2,2,2,2,24,1056]{5,4,3,2,1,0:T(8,128)(2,1)} %copy-done.5, bf16[2,2,2,2,24,1056]{5,4,3,2,1,0:T(8,128)(2,1)} %pad_maximum_fusion.1.refs_1_, bf16[2,2,2,2,24,1056]{5,4,3,2,1,0:T(8,128)(2,1)} %copy-done.6, ...), custom_call_target="tpu_custom_call" | custom-call | flops 1 | bytes 1 | tf_op jit(solution)/shard_map/arranged/pallas_call | solution.py:113
  97.1 7.2 %products.5 = f32[4,192,512]{2,1,0:T(8,128)} custom-call(s32[9]{0:T(128)} %get-tuple-element.167.table_ref, bf16[8,4,192,264]{3,2,1,0:T(8,128)(2,1)} %arranged.2.rows_ref, f32[4,264,2048]{2,1,0:T(8,128)} %refs_2_.19, bf16[4,264,512]{2,1,0:T(8,128)(2,1)} %copy-done.8, bf16[4,264,512]{2,1,0:T(8,128)(2,1)} %copy-done.9, ...), custom_call_target="tpu_custom_call" | custom-call | flops 1 | bytes 1 | tf_op jit(solution)/shard_map/products/pallas_call | solution.py:156
  104.3 7.7 %collective-permute-done.15.refs_1_ = bf16[4,264,512]{2,1,0:T(8,128)(2,1)} collective-permute-done((bf16[4,264,512]{2,1,0:T(8,128)(2,1)}, bf16[4,264,512]{2,1,0:T(8,128)(2,1)}, u32[]{:S(2)}, u32[]{:S(2)}) %collective-permute-start.15) | collective-permute-done | bytes 1081376 | tf_op jit(solution)/shard_map/ppermute | solution.py:287
  112.2 1.5 collective-permute-start.17
  113.8 1.6 collective-permute-start.18
  117.2 7.2 %products.4 = f32[4,192,512]{2,1,0:T(8,128)} custom-call(s32[9]{0:T(128)} %get-tuple-element.165.table_ref, bf16[8,4,192,264]{3,2,1,0:T(8,128)(2,1)} %arranged.2.rows_ref, f32[4,264,2048]{2,1,0:T(8,128)} %refs_2_.19, bf16[4,264,512]{2,1,0:T(8,128)(2,1)} %copy-done.8, bf16[4,264,512]{2,1,0:T(8,128)(2,1)} %copy-done.9, ...), custom_call_target="tpu_custom_call" | custom-call | flops 1 | bytes 1 | tf_op jit(solution)/shard_map/products/pallas_call | solution.py:156
  124.4 8.9 %arranged.3.rows_ref = bf16[8,4,192,264]{3,2,1,0:T(8,128)(2,1)} custom-call(s32[3]{0:T(128)} %pad_add_fusion.table_ref, bf16[2,2,2,2,24,1056]{5,4,3,2,1,0:T(8,128)(2,1)} %copy-done.5, bf16[2,2,2,2,24,1056]{5,4,3,2,1,0:T(8,128)(2,1)} %pad_maximum_fusion.1.refs_1_, bf16[2,2,2,2,24,1056]{5,4,3,2,1,0:T(8,128)(2,1)} %copy-done.6, ...), custom_call_target="tpu_custom_call" | custom-call | flops 1 | bytes 1 | tf_op jit(solution)/shard_map/arranged/pallas_call | solution.py:113
  133.3 27.2 %collective-permute-done.17.refs_0_ = bf16[4,264,512]{2,1,0:T(8,128)(2,1)S(1)} collective-permute-done((bf16[4,264,512]{2,1,0:T(8,128)(2,1)}, bf16[4,264,512]{2,1,0:T(8,128)(2,1)S(1)}, u32[]{:S(2)}, u32[]{:S(2)}) %collective-permute-start.17) | collective-permute-done | bytes 1081376 | tf_op jit(solution)/shard_map/ppermute | solution.py:287
  160.6 8.5 %collective-permute-done.18.refs_2_ = bf16[4,264,512]{2,1,0:T(8,128)(2,1)} collective-permute-done((bf16[4,264,512]{2,1,0:T(8,128)(2,1)}, bf16[4,264,512]{2,1,0:T(8,128)(2,1)}, u32[]{:S(2)}, u32[]{:S(2)}) %collective-permute-start.18) | collective-permute-done | bytes 1081376 | tf_op jit(solution)/shard_map/ppermute | solution.py:287
  169.1 7.2 %products.6 = f32[4,192,512]{2,1,0:T(8,128)} custom-call(s32[9]{0:T(128)} %get-tuple-element.166.table_ref, bf16[8,4,192,264]{3,2,1,0:T(8,128)(2,1)} %arranged.3.rows_ref, f32[4,264,2048]{2,1,0:T(8,128)} %refs_2_.15, bf16[4,264,512]{2,1,0:T(8,128)(2,1)} %copy-done.10, bf16[4,264,512]{2,1,0:T(8,128)(2,1)} %collective-permute-done.15.refs_1_, ...), custom_call_target="tpu_custom_call" | custom-call | flops 1 | bytes 1 | tf_op jit(solution)/shard_map/products/pallas_call | solution.py:156
  176.3 6.1 %collective-permute-done.16 = f32[4,192,512]{2,1,0:T(8,128)S(1)} collective-permute-done((f32[4,192,512]{2,1,0:T(8,128)}, f32[4,192,512]{2,1,0:T(8,128)S(1)}, u32[]{:S(2)}, u32[]{:S(2)}) %collective-permute-start.16) | collective-permute-done | bytes 1572896 | tf_op jit(solution)/shard_map/ppermute | solution.py:292
  182.4 1.7 slice.26
  184.9 7.1 %psum.14 = f32[4,192]{1,0:T(4,128)S(1)} all-reduce(f32[4,192]{1,0:T(4,128)S(1)} %multiply_reduce_fusion.1), channel_id=1, replica_groups=mesh['path'=8,'shard'=4] {'shard'}, use_global_device_ids=true, to_apply=%region_8.10 | all-reduce | flops 768 | bytes 6144 | tf_op jit(solution)/shard_map/psum | solution.py:369
  192.0 1.7 collective-permute-start.19
  193.7 7.9 %collective-permute-done.19 = f32[4,192]{1,0:T(4,128)S(1)} collective-permute-done((f32[4,192]{1,0:T(4,128)S(1)}, f32[4,192]{1,0:T(4,128)S(1)}, u32[]{:S(2)}, u32[]{:S(2)}) %collective-permute-start.19) | collective-permute-done | bytes 3104 | tf_op jit(solution)/shard_map/ppermute | solution.py:287
  201.6 1.5 collective-permute-start.20
  203.1 2.1 collective-permute-done.20
  205.2 2.5 broadcast_divide_fusion
  207.7 12.4 %collective-permute-done.21 = f32[2,192,512]{2,1,0:T(8,128)S(1)} collective-permute-done((f32[2,192,512]{2,1,0:T(8,128)S(1)}, f32[2,192,512]{2,1,0:T(8,128)S(1)}, u32[]{:S(2)}, u32[]{:S(2)}) %collective-permute-start.21) | collective-permute-done | bytes 786464 | tf_op jit(solution)/shard_map/ppermute | solution.py:292
  220.2 1.6 collective-permute-start.24
  221.8 3.0 collective-permute-start.22
  224.8 7.3 %products.7 = f32[4,192,512]{2,1,0:T(8,128)} custom-call(s32[9]{0:T(128)} %get-tuple-element.164.table_ref, bf16[8,4,192,264]{3,2,1,0:T(8,128)(2,1)} %arranged.3.rows_ref, f32[4,264,2048]{2,1,0:T(8,128)} %refs_2_.15, bf16[4,264,512]{2,1,0:T(8,128)(2,1)} %copy-done.10, bf16[4,264,512]{2,1,0:T(8,128)(2,1)} %collective-permute-done.15.refs_1_, ...), custom_call_target="tpu_custom_call" | custom-call | flops 1 | bytes 1 | tf_op jit(solution)/shard_map/products/pallas_call | solution.py:156
  232.1 7.6 %collective-permute-done.24.refs_0_ = bf16[4,192,512]{2,1,0:T(8,128)(2,1)S(1)} collective-permute-done((bf16[4,192,512]{2,1,0:T(8,128)(2,1)S(1)}, bf16[4,192,512]{2,1,0:T(8,128)(2,1)S(1)}, u32[]{:S(2)}, u32[]{:S(2)}) %collective-permute-start.24) | collective-permute-done | bytes 786464 | tf_op jit(solution)/shard_map/ppermute | solution.py:287
  239.7 18.0 %collective-permute-done.23.refs_0_ = bf16[4,192,512]{2,1,0:T(8,128)(2,1)} collective-permute-done((bf16[4,192,512]{2,1,0:T(8,128)(2,1)S(1)}, bf16[4,192,512]{2,1,0:T(8,128)(2,1)}, u32[]{:S(2)}, u32[]{:S(2)}) %collective-permute-start.23) | collective-permute-done | bytes 786464 | tf_op jit(solution)/shard_map/ppermute | solution.py:287
  262.3 2.6 collective-permute-start.28
  266.7 2.4 constant_dynamic-slice_fusion.1
  269.1 2.4 copy.32
  271.6 2.4 constant_dynamic-slice_fusion
  274.0 2.4 copy.33
  276.4 7.6 %updated.8 = (f32[4,264,2048]{2,1,0:T(8,128)}, bf16[4,264,2048]{2,1,0:T(8,128)(2,1)}) custom-call(s32[11]{0:T(128)} %get-tuple-element.161.table_ref, bf16[8,264,192]{2,1,0:T(8,128)(2,1)} %bitcast.46, bf16[4,192,512]{2,1,0:T(8,128)(2,1)} %copy-done.14, bf16[4,192,512]{2,1,0:T(8,128)(2,1)} %collective-permute-done.22.refs_1_, f32[4,264,2048]{2,1,0:T(8,128)} %refs_2_.15, ...), custom_call_target="tpu_custom_call" | custom-call | flops 1 | bytes 1 | tf_op jit(solution)/shard_map/updated/pallas_call | solution.py:235
  284.0 9.3 %collective-permute-done.26.refs_1_ = bf16[4,192,512]{2,1,0:T(8,128)(2,1)} collective-permute-done((bf16[4,192,512]{2,1,0:T(8,128)(2,1)}, bf16[4,192,512]{2,1,0:T(8,128)(2,1)}, u32[]{:S(2)}, u32[]{:S(2)}) %collective-permute-start.26) | collective-permute-done | bytes 786464 | tf_op jit(solution)/shard_map/ppermute | solution.py:287
  293.4 4.6 %collective-permute-done.28 = f32[2,192,512]{2,1,0:T(8,128)S(1)} collective-permute-done((f32[2,192,512]{2,1,0:T(8,128)}, f32[2,192,512]{2,1,0:T(8,128)S(1)}, u32[]{:S(2)}, u32[]{:S(2)}) %collective-permute-start.28) | collective-permute-done | bytes 786464 | tf_op jit(solution)/shard_map/ppermute | solution.py:292
  298.9 5.6 %psum.15 = f32[4,192]{1,0:T(4,128)S(1)} all-reduce(f32[4,192]{1,0:T(4,128)S(1)} %multiply_reduce_fusion), channel_id=1, replica_groups=mesh['path'=8,'shard'=4] {'shard'}, use_global_device_ids=true, to_apply=%region_10.12 | all-reduce | flops 768 | bytes 6144 | tf_op jit(solution)/shard_map/psum | solution.py:369
  304.6 3.6 collective-permute-done.29
  310.3 1.7 collective-permute-done.30
  311.9 3.2 fusion.6.refs_0_
  315.7 7.5 %updated.9 = (f32[4,264,2048]{2,1,0:T(8,128)}, bf16[4,264,2048]{2,1,0:T(8,128)(2,1)}) custom-call(s32[11]{0:T(128)} %get-tuple-element.158.table_ref, bf16[8,264,192]{2,1,0:T(8,128)(2,1)} %bitcast.47, bf16[4,192,512]{2,1,0:T(8,128)(2,1)} %collective-permute-done.23.refs_0_, ...), custom_call_target="tpu_custom_call", output_to_operand_aliasing={{0}: (6, {}), {1}: (7, {})} | custom-call | flops 1 | bytes 1 | tf_op jit(solution)/shard_map/updated/pallas_call | solution.py:235
  323.2 2.7 collective-permute-start.31
  325.9 3.6 collective-permute-done.32.refs_1_
  329.4 14.3 %collective-permute-done.34.refs_0_ = bf16[4,192,512]{2,1,0:T(8,128)(2,1)S(1)} collective-permute-done((bf16[4,192,512]{2,1,0:T(8,128)(2,1)S(1)}, bf16[4,192,512]{2,1,0:T(8,128)(2,1)S(1)}, u32[]{:S(2)}, u32[]{:S(2)}) %collective-permute-start.34) | collective-permute-done | bytes 786464 | tf_op jit(solution)/shard_map/ppermute | solution.py:287
  343.7 1.6 collective-permute-start.35
  345.3 7.5 %updated.10 = (f32[4,264,2048]{2,1,0:T(8,128)}, bf16[4,264,2048]{2,1,0:T(8,128)(2,1)}) custom-call(s32[11]{0:T(128)} %get-tuple-element.157.table_ref, bf16[8,264,192]{2,1,0:T(8,128)(2,1)} %bitcast.48, bf16[4,192,512]{2,1,0:T(8,128)(2,1)} %copy-done.16, ...), custom_call_target="tpu_custom_call", output_to_operand_aliasing={{0}: (6, {}), {1}: (7, {})} | custom-call | flops 1 | bytes 1 | tf_op jit(solution)/shard_map/updated/pallas_call | solution.py:235
  352.8 7.5 %updated.11 = (f32[4,264,2048]{2,1,0:T(8,128)}, bf16[4,264,2048]{2,1,0:T(8,128)(2,1)}) custom-call(s32[11]{0:T(128)} %get-tuple-element.159.table_ref, bf16[8,264,192]{2,1,0:T(8,128)(2,1)} %bitcast.49, bf16[4,192,512]{2,1,0:T(8,128)(2,1)} %collective-permute-done.27.refs_0_, ...), custom_call_target="tpu_custom_call", output_to_operand_aliasing={{0}: (6, {}), {1}: (7, {})} | custom-call | flops 1 | bytes 1 | tf_op jit(solution)/shard_map/updated/pallas_call | solution.py:235
  361.2 1.8 collective-permute-start.36
  363.3 7.4 %updated.12 = (f32[4,264,2048]{2,1,0:T(8,128)}, bf16[4,264,2048]{2,1,0:T(8,128)(2,1)}) custom-call(s32[11]{0:T(128)} %get-tuple-element.162.table_ref, bf16[8,264,192]{2,1,0:T(8,128)(2,1)} %bitcast.42, bf16[4,192,512]{2,1,0:T(8,128)(2,1)} %copy-done.13, bf16[4,192,512]{2,1,0:T(8,128)(2,1)} %copy-done.20, f32[4,264,2048]{2,1,0:T(8,128)} %refs_2_.19, ...), custom_call_target="tpu_custom_call" | custom-call | flops 1 | bytes 1 | tf_op jit(solution)/shard_map/updated/pallas_call | solution.py:235
  370.8 6.9 %collective-permute-done.36.refs_1_ = bf16[4,192,512]{2,1,0:T(8,128)(2,1)S(1)} collective-permute-done((bf16[4,192,512]{2,1,0:T(8,128)(2,1)S(1)}, bf16[4,192,512]{2,1,0:T(8,128)(2,1)S(1)}, u32[]{:S(2)}, u32[]{:S(2)}) %collective-permute-start.36) | collective-permute-done | bytes 786464 | tf_op jit(solution)/shard_map/ppermute | solution.py:287
  380.8 7.5 %updated.13 = (f32[4,264,2048]{2,1,0:T(8,128)}, bf16[4,264,2048]{2,1,0:T(8,128)(2,1)}) custom-call(s32[11]{0:T(128)} %get-tuple-element.143.table_ref, bf16[8,264,192]{2,1,0:T(8,128)(2,1)} %bitcast.43, bf16[4,192,512]{2,1,0:T(8,128)(2,1)} %copy-done.18, bf16[4,192,512]{2,1,0:T(8,128)(2,1)} %copy-done.24, ...), custom_call_target="tpu_custom_call", output_to_operand_aliasing={{0}: (6, {}), {1}: (7, {})} | custom-call | flops 1 | bytes 1 | tf_op jit(solution)/shard_map/updated/pallas_call | solution.py:235
  388.2 7.5 %updated.14 = (f32[4,264,2048]{2,1,0:T(8,128)}, bf16[4,264,2048]{2,1,0:T(8,128)(2,1)}) custom-call(s32[11]{0:T(128)} %get-tuple-element.145.table_ref, bf16[8,264,192]{2,1,0:T(8,128)(2,1)} %bitcast.44, bf16[4,192,512]{2,1,0:T(8,128)(2,1)} %copy-done.17, bf16[4,192,512]{2,1,0:T(8,128)(2,1)} %copy-done.22, ...), custom_call_target="tpu_custom_call", output_to_operand_aliasing={{0}: (6, {}), {1}: (7, {})} | custom-call | flops 1 | bytes 1 | tf_op jit(solution)/shard_map/updated/pallas_call | solution.py:235
  396.6 7.6 %updated.15 = (f32[4,264,2048]{2,1,0:T(8,128)}, bf16[4,264,2048]{2,1,0:T(8,128)(2,1)}) custom-call(s32[11]{0:T(128)} %pad_add_fusion.10.table_ref, bf16[8,264,192]{2,1,0:T(8,128)(2,1)} %bitcast.45, bf16[4,192,512]{2,1,0:T(8,128)(2,1)} %copy-done.19, bf16[4,192,512]{2,1,0:T(8,128)(2,1)} %copy-done.23, ...), custom_call_target="tpu_custom_call", output_to_operand_aliasing={{0}: (6, {}), {1}: (7, {})} | custom-call | flops 1 | bytes 1 | tf_op jit(solution)/shard_map/updated/pallas_call | solution.py:235
  (151 shorter events, 36.9 us)
Async XLA Ops:
  0.6 13.2 %copy-start = (bf16[192,2112]{1,0:T(8,128)(2,1)S(1)}, bf16[192,2112]{1,0:T(8,128)(2,1)}, u32[]{:S(2)}) copy-start(bf16[192,2112]{1,0:T(8,128)(2,1)} %param.11) | copy-start | bytes 2433028
  0.7 9.6 %copy-start.27 = (s32[1,24]{1,0:T(1,128)S(1)}, s32[1,24]{1,0:T(1,128)}, u32[]{:S(2)}) copy-start(s32[1,24]{1,0:T(1,128)} %param.13) | copy-start | bytes 292
  0.7 9.9 %copy-start.28 = (s32[1,24]{1,0:T(1,128)S(1)}, s32[1,24]{1,0:T(1,128)}, u32[]{:S(2)}) copy-start(s32[1,24]{1,0:T(1,128)} %param.14) | copy-start | bytes 292
  5.7 46.6 %collective-permute-start.4 = (bf16[4,264,512]{2,1,0:T(8,128)(2,1)}, bf16[4,264,512]{2,1,0:T(8,128)(2,1)S(1)}, u32[]{:S(2)}, u32[]{:S(2)}) collective-permute-start(bf16[4,264,512]{2,1,0:T(8,128)(2,1)} %get-tuple-element.74), channel_id=1, source_target_pairs={{0,4},{4,0},{8,12},{12,8},{16,20},{20,16},{24,28},{28,24},{1,5},{5... | collective-permute-start | bytes 3244040 | tf_op jit(solution)/shard_map/ppermute | solution.py:287
  8.7 43.7 %collective-permute-start.5 = (bf16[4,264,512]{2,1,0:T(8,128)(2,1)}, bf16[4,264,512]{2,1,0:T(8,128)(2,1)S(1)}, u32[]{:S(2)}, u32[]{:S(2)}) collective-permute-start(bf16[4,264,512]{2,1,0:T(8,128)(2,1)} %get-tuple-element.75), channel_id=1, source_target_pairs={{0,8},{4,12},{8,0},{12,4},{16,24},{20,28},{24,16},{28,20},{1,9},{5... | collective-permute-start | bytes 3244040 | tf_op jit(solution)/shard_map/ppermute | solution.py:287
  14.3 41.7 %copy-start.26 = (s32[8,2]{0,1:T(2,128)S(1)}, s32[8,2]{0,1:T(2,128)}, u32[]{:S(2)}) copy-start(s32[8,2]{0,1:T(2,128)} %param.15) | copy-start | bytes 196
  15.6 22.4 %collective-permute-start = (bf16[2,2,24,1056]{3,2,1,0:T(8,128)(2,1)S(1)}, bf16[2,2,24,1056]{3,2,1,0:T(8,128)(2,1)S(1)}, u32[]{:S(2)}, u32[]{:S(2)}) collective-permute-start(bf16[2,2,24,1056]{3,2,1,0:T(8,128)(2,1)S(1)} %get-tuple-element.154), channel_id=1, source_target_pairs={{0,16},{4,20},{8,24},{12,28},{16,0},{20,4},{24,8},{28,12},{1,17},{... | collective-permute-start | bytes 608264 | tf_op jit(solution)/shard_map/ppermute | solution.py:292
  38.1 10.9 %collective-permute-start.2 = (bf16[2,2,2,24,1056]{4,3,2,1,0:T(8,128)(2,1)S(1)}, bf16[2,2,2,24,1056]{4,3,2,1,0:T(8,128)(2,1)}, u32[]{:S(2)}, u32[]{:S(2)}) collective-permute-start(bf16[2,2,2,24,1056]{4,3,2,1,0:T(8,128)(2,1)S(1)} %get-tuple-element.152), channel_id=1, source_target_pairs={{0,4},{4,0},{8,12},{12,8},{16,20},{20,16},{24,28},{28,24},{1,5},{5... | collective-permute-start | bytes 1216520 | tf_op jit(solution)/shard_map/ppermute | solution.py:287
  38.7 12.3 %collective-permute-start.1 = (bf16[2,2,2,24,1056]{4,3,2,1,0:T(8,128)(2,1)S(1)}, bf16[2,2,2,24,1056]{4,3,2,1,0:T(8,128)(2,1)}, u32[]{:S(2)}, u32[]{:S(2)}) collective-permute-start(bf16[2,2,2,24,1056]{4,3,2,1,0:T(8,128)(2,1)S(1)} %get-tuple-element.152), channel_id=1, source_target_pairs={{0,8},{4,12},{8,0},{12,4},{16,24},{20,28},{24,16},{28,20},{1,9},{5... | collective-permute-start | bytes 1216520 | tf_op jit(solution)/shard_map/ppermute | solution.py:287
  42.2 10.2 %collective-permute-start.3 = (bf16[2,2,2,24,1056]{4,3,2,1,0:T(8,128)(2,1)S(1)}, bf16[2,2,2,24,1056]{4,3,2,1,0:T(8,128)(2,1)S(1)}, u32[]{:S(2)}, u32[]{:S(2)}) collective-permute-start(bf16[2,2,2,24,1056]{4,3,2,1,0:T(8,128)(2,1)S(1)} %get-tuple-element.152), channel_id=1, source_target_pairs={{0,2},{1,3},{2,0},{3,1},{4,6},{5,7},{6,4},{7,5},{8,10},{9,11},{10,... | collective-permute-start | bytes 1216520 | tf_op jit(solution)/shard_map/ppermute | solution.py:297
  52.3 3.6 copy-start.25
  52.3 10.1 %copy-start.8 = (bf16[4,264,512]{2,1,0:T(8,128)(2,1)}, bf16[4,264,512]{2,1,0:T(8,128)(2,1)S(1)}, u32[]{:S(2)}) copy-start(bf16[4,264,512]{2,1,0:T(8,128)(2,1)S(1)} %collective-permute-done.4.refs_0_) | copy-start | bytes 3244036
  52.4 3.6 copy-start.9
  52.4 19.9 %collective-permute-start.7 = (bf16[2,2,2,24,1056]{4,3,2,1,0:T(8,128)(2,1)}, bf16[2,2,2,24,1056]{4,3,2,1,0:T(8,128)(2,1)}, u32[]{:S(2)}, u32[]{:S(2)}) collective-permute-start(bf16[2,2,2,24,1056]{4,3,2,1,0:T(8,128)(2,1)} %collective-permute-done.1), channel_id=1, source_target_pairs={{0,2},{1,3},{2,0},{3,1},{4,6},{5,7},{6,4},{7,5},{8,10},{9,11},{10,... | collective-permute-start | bytes 1216520 | tf_op jit(solution)/shard_map/ppermute | solution.py:297
  53.9 18.3 %collective-permute-start.6 = (bf16[2,2,2,24,1056]{4,3,2,1,0:T(8,128)(2,1)}, bf16[2,2,2,24,1056]{4,3,2,1,0:T(8,128)(2,1)}, u32[]{:S(2)}, u32[]{:S(2)}) collective-permute-start(bf16[2,2,2,24,1056]{4,3,2,1,0:T(8,128)(2,1)} %collective-permute-done.1), channel_id=1, source_target_pairs={{0,4},{4,0},{8,12},{12,8},{16,20},{20,16},{24,28},{28,24},{1,5},{5... | collective-permute-start | bytes 1216520 | tf_op jit(solution)/shard_map/ppermute | solution.py:287
  55.4 16.8 %collective-permute-start.8 = (bf16[2,2,2,24,1056]{4,3,2,1,0:T(8,128)(2,1)}, bf16[2,2,2,24,1056]{4,3,2,1,0:T(8,128)(2,1)}, u32[]{:S(2)}, u32[]{:S(2)}) collective-permute-start(bf16[2,2,2,24,1056]{4,3,2,1,0:T(8,128)(2,1)} %collective-permute-done.2), channel_id=1, source_target_pairs={{0,2},{1,3},{2,0},{3,1},{4,6},{5,7},{6,4},{7,5},{8,10},{9,11},{10,... | collective-permute-start | bytes 1216520 | tf_op jit(solution)/shard_map/ppermute | solution.py:297
  57.1 5.3 %copy-start.5 = (bf16[2,2,2,2,24,1056]{5,4,3,2,1,0:T(8,128)(2,1)}, bf16[2,2,2,2,24,1056]{5,4,3,2,1,0:T(8,128)(2,1)S(1)}, u32[]{:S(2)}) copy-start(bf16[2,2,2,2,24,1056]{5,4,3,2,1,0:T(8,128)(2,1)S(1)} %pad_maximum_fusion.refs_0_) | copy-start | bytes 2433028
  57.1 26.5 %collective-permute-start.10 = (bf16[2,2,2,2,24,1056]{5,4,3,2,1,0:T(8,128)(2,1)S(1)}, bf16[2,2,2,2,24,1056]{5,4,3,2,1,0:T(8,128)(2,1)S(1)}, u32[]{:S(2)}, u32[]{:S(2)}) collective-permute-start(bf16[2,2,2,2,24,1056]{5,4,3,2,1,0:T(8,128)(2,1)S(1)} %pad_maximum_fusion.refs_0_), channel_id=1, source_target_pairs={{0,1},{1,0},{2,3},{3,2},{4,5},{5,4},{6,7},{7,6},{8,9},{9,8},{10,11... | collective-permute-start | bytes 2433032 | tf_op jit(solution)/shard_map/ppermute | solution.py:297
  62.4 34.7 %collective-permute-start.14 = (bf16[4,264,512]{2,1,0:T(8,128)(2,1)}, bf16[4,264,512]{2,1,0:T(8,128)(2,1)}, u32[]{:S(2)}, u32[]{:S(2)}) collective-permute-start(bf16[4,264,512]{2,1,0:T(8,128)(2,1)} %get-tuple-element.88), channel_id=1, source_target_pairs={{0,12},{4,8},{8,4},{12,0},{16,28},{20,24},{24,20},{28,16},{1,13},{... | collective-permute-start | bytes 3244040 | tf_op jit(solution)/shard_map/ppermute | solution.py:287
  72.2 8.7 %collective-permute-start.9 = (bf16[2,2,2,24,1056]{4,3,2,1,0:T(8,128)(2,1)}, bf16[2,2,2,24,1056]{4,3,2,1,0:T(8,128)(2,1)S(1)}, u32[]{:S(2)}, u32[]{:S(2)}) collective-permute-start(bf16[2,2,2,24,1056]{4,3,2,1,0:T(8,128)(2,1)} %collective-permute-done.6), channel_id=1, source_target_pairs={{0,2},{1,3},{2,0},{3,1},{4,6},{5,7},{6,4},{7,5},{8,10},{9,11},{10,... | collective-permute-start | bytes 1216520 | tf_op jit(solution)/shard_map/ppermute | solution.py:297
  75.0 8.7 %copy-start.6 = (bf16[2,2,2,2,24,1056]{5,4,3,2,1,0:T(8,128)(2,1)}, bf16[2,2,2,2,24,1056]{5,4,3,2,1,0:T(8,128)(2,1)S(1)}, u32[]{:S(2)}) copy-start(bf16[2,2,2,2,24,1056]{5,4,3,2,1,0:T(8,128)(2,1)S(1)} %pad_maximum_fusion.2.refs_2_) | copy-start | bytes 2433028
  75.0 12.1 %collective-permute-start.12 = (bf16[2,2,2,2,24,1056]{5,4,3,2,1,0:T(8,128)(2,1)S(1)}, bf16[2,2,2,2,24,1056]{5,4,3,2,1,0:T(8,128)(2,1)}, u32[]{:S(2)}, u32[]{:S(2)}) collective-permute-start(bf16[2,2,2,2,24,1056]{5,4,3,2,1,0:T(8,128)(2,1)S(1)} %pad_maximum_fusion.2.refs_2_), channel_id=1, source_target_pairs={{0,1},{1,0},{2,3},{3,2},{4,5},{5,4},{6,7},{7,6},{8,9},{9,8},{10,11... | collective-permute-start | bytes 2433032 | tf_op jit(solution)/shard_map/ppermute | solution.py:297
  77.5 9.6 %collective-permute-start.11 = (bf16[2,2,2,2,24,1056]{5,4,3,2,1,0:T(8,128)(2,1)}, bf16[2,2,2,2,24,1056]{5,4,3,2,1,0:T(8,128)(2,1)}, u32[]{:S(2)}, u32[]{:S(2)}) collective-permute-start(bf16[2,2,2,2,24,1056]{5,4,3,2,1,0:T(8,128)(2,1)} %pad_maximum_fusion.1.refs_1_), channel_id=1, source_target_pairs={{0,1},{1,0},{2,3},{3,2},{4,5},{5,4},{6,7},{7,6},{8,9},{9,8},{10,11... | collective-permute-start | bytes 2433032 | tf_op jit(solution)/shard_map/ppermute | solution.py:297
  80.9 31.0 %collective-permute-start.15 = (bf16[4,264,512]{2,1,0:T(8,128)(2,1)}, bf16[4,264,512]{2,1,0:T(8,128)(2,1)}, u32[]{:S(2)}, u32[]{:S(2)}) collective-permute-start(bf16[4,264,512]{2,1,0:T(8,128)(2,1)} %get-tuple-element.90), channel_id=1, source_target_pairs={{0,8},{4,12},{8,0},{12,4},{16,24},{20,28},{24,16},{28,20},{1,9},{5... | collective-permute-start | bytes 3244040 | tf_op jit(solution)/shard_map/ppermute | solution.py:287
  84.6 2.6 collective-permute-start.13
  87.2 0.9 copy-start.12
  111.9 70.4 %collective-permute-start.16 = (f32[4,192,512]{2,1,0:T(8,128)}, f32[4,192,512]{2,1,0:T(8,128)S(1)}, u32[]{:S(2)}, u32[]{:S(2)}) collective-permute-start(f32[4,192,512]{2,1,0:T(8,128)} %products.5), channel_id=1, source_target_pairs={{0,16},{4,20},{8,24},{12,28},{16,0},{20,4},{24,8},{28,12},{1,17},{... | collective-permute-start | bytes 4718600 | tf_op jit(solution)/shard_map/ppermute | solution.py:292
  112.2 48.3 %collective-permute-start.17 = (bf16[4,264,512]{2,1,0:T(8,128)(2,1)}, bf16[4,264,512]{2,1,0:T(8,128)(2,1)S(1)}, u32[]{:S(2)}, u32[]{:S(2)}) collective-permute-start(bf16[4,264,512]{2,1,0:T(8,128)(2,1)} %get-tuple-element.93), channel_id=1, source_target_pairs={{0,4},{4,0},{8,12},{12,8},{16,20},{20,16},{24,28},{28,24},{1,5},{5... | collective-permute-start | bytes 3244040 | tf_op jit(solution)/shard_map/ppermute | solution.py:287
  113.8 55.3 %collective-permute-start.18 = (bf16[4,264,512]{2,1,0:T(8,128)(2,1)}, bf16[4,264,512]{2,1,0:T(8,128)(2,1)}, u32[]{:S(2)}, u32[]{:S(2)}) collective-permute-start(bf16[4,264,512]{2,1,0:T(8,128)(2,1)} %get-tuple-element.95), channel_id=1, source_target_pairs={{0,12},{4,8},{8,4},{12,0},{16,28},{20,24},{24,20},{28,16},{1,13},{... | collective-permute-start | bytes 3244040 | tf_op jit(solution)/shard_map/ppermute | solution.py:287
  160.6 8.5 %copy-start.10 = (bf16[4,264,512]{2,1,0:T(8,128)(2,1)}, bf16[4,264,512]{2,1,0:T(8,128)(2,1)S(1)}, u32[]{:S(2)}) copy-start(bf16[4,264,512]{2,1,0:T(8,128)(2,1)S(1)} %collective-permute-done.17.refs_0_) | copy-start | bytes 3244036
  176.3 7.9 %copy-start.2 = (f32[4,192,512]{2,1,0:T(8,128)S(1)}, f32[4,192,512]{2,1,0:T(8,128)}, u32[]{:S(2)}) copy-start(f32[4,192,512]{2,1,0:T(8,128)} %products.4) | copy-start | bytes 4718596
  182.4 2.6 copy-start.3
  184.1 36.0 %collective-permute-start.21 = (f32[2,192,512]{2,1,0:T(8,128)S(1)}, f32[2,192,512]{2,1,0:T(8,128)S(1)}, u32[]{:S(2)}, u32[]{:S(2)}) collective-permute-start(f32[2,192,512]{2,1,0:T(8,128)S(1)} %slice.26), channel_id=1, source_target_pairs={{0,16},{4,20},{8,24},{12,28},{16,0},{20,4},{24,8},{28,12},{1,17},{... | collective-permute-start | bytes 2359304 | tf_op jit(solution)/shard_map/ppermute | solution.py:292
  192.0 9.6 %collective-permute-start.19 = (f32[4,192]{1,0:T(4,128)S(1)}, f32[4,192]{1,0:T(4,128)S(1)}, u32[]{:S(2)}, u32[]{:S(2)}) collective-permute-start(f32[4,192]{1,0:T(4,128)S(1)} %psum.14), channel_id=1, source_target_pairs={{0,8},{4,12},{8,0},{12,4},{16,24},{20,28},{24,16},{28,20},{1,9},{5... | collective-permute-start | bytes 9224 | tf_op jit(solution)/shard_map/ppermute | solution.py:287
  201.6 3.6 collective-permute-start.20
  220.2 11.9 %copy-start.14 = (bf16[4,192,512]{2,1,0:T(8,128)(2,1)}, bf16[4,192,512]{2,1,0:T(8,128)(2,1)S(1)}, u32[]{:S(2)}) copy-start(bf16[4,192,512]{2,1,0:T(8,128)(2,1)S(1)} %convert_element_type.21.refs_0_) | copy-start | bytes 2359300
  220.2 19.5 %collective-permute-start.24 = (bf16[4,192,512]{2,1,0:T(8,128)(2,1)S(1)}, bf16[4,192,512]{2,1,0:T(8,128)(2,1)S(1)}, u32[]{:S(2)}, u32[]{:S(2)}) collective-permute-start(bf16[4,192,512]{2,1,0:T(8,128)(2,1)S(1)} %convert_element_type.21.refs_0_), channel_id=1, source_target_pairs={{0,4},{4,0},{8,12},{12,8},{16,20},{20,16},{24,28},{28,24},{1,5},{5... | collective-permute-start | bytes 2359304 | tf_op jit(solution)/shard_map/ppermute | solution.py:287
  221.8 35.9 %collective-permute-start.23 = (bf16[4,192,512]{2,1,0:T(8,128)(2,1)S(1)}, bf16[4,192,512]{2,1,0:T(8,128)(2,1)}, u32[]{:S(2)}, u32[]{:S(2)}) collective-permute-start(bf16[4,192,512]{2,1,0:T(8,128)(2,1)S(1)} %convert_element_type.21.refs_0_), channel_id=1, source_target_pairs={{0,8},{4,12},{8,0},{12,4},{16,24},{20,28},{24,16},{28,20},{1,9},{5... | collective-permute-start | bytes 2359304 | tf_op jit(solution)/shard_map/ppermute | solution.py:287
  221.8 37.2 %collective-permute-start.22 = (bf16[4,192,512]{2,1,0:T(8,128)(2,1)S(1)}, bf16[4,192,512]{2,1,0:T(8,128)(2,1)}, u32[]{:S(2)}, u32[]{:S(2)}) collective-permute-start(bf16[4,192,512]{2,1,0:T(8,128)(2,1)S(1)} %convert_element_type.21.refs_0_), channel_id=1, source_target_pairs={{0,16},{4,20},{8,24},{12,28},{16,0},{20,4},{24,8},{28,12},{1,17},{... | collective-permute-start | bytes 2359304 | tf_op jit(solution)/shard_map/ppermute | solution.py:292
  224.8 36.5 %copy-start.7 = (f32[4,192,512]{2,1,0:T(8,128)S(1)}, f32[4,192,512]{2,1,0:T(8,128)}, u32[]{:S(2)}) copy-start(f32[4,192,512]{2,1,0:T(8,128)} %products.6) | copy-start | bytes 4718596
  239.7 22.6 %copy-start.16 = (bf16[4,192,512]{2,1,0:T(8,128)(2,1)}, bf16[4,192,512]{2,1,0:T(8,128)(2,1)S(1)}, u32[]{:S(2)}) copy-start(bf16[4,192,512]{2,1,0:T(8,128)(2,1)S(1)} %collective-permute-done.24.refs_0_) | copy-start | bytes 2359300
  259.0 25.0 %collective-permute-start.27 = (bf16[4,192,512]{2,1,0:T(8,128)(2,1)}, bf16[4,192,512]{2,1,0:T(8,128)(2,1)}, u32[]{:S(2)}, u32[]{:S(2)}) collective-permute-start(bf16[4,192,512]{2,1,0:T(8,128)(2,1)} %collective-permute-done.23.refs_0_), channel_id=1, source_target_pairs={{0,4},{4,0},{8,12},{12,8},{16,20},{20,16},{24,28},{28,24},{1,5},{5... | collective-permute-start | bytes 2359304 | tf_op jit(solution)/shard_map/ppermute | solution.py:287
  259.5 33.8 %collective-permute-start.26 = (bf16[4,192,512]{2,1,0:T(8,128)(2,1)}, bf16[4,192,512]{2,1,0:T(8,128)(2,1)}, u32[]{:S(2)}, u32[]{:S(2)}) collective-permute-start(bf16[4,192,512]{2,1,0:T(8,128)(2,1)} %collective-permute-done.22.refs_1_), channel_id=1, source_target_pairs={{0,4},{4,0},{8,12},{12,8},{16,20},{20,16},{24,28},{28,24},{1,5},{5... | collective-permute-start | bytes 2359304 | tf_op jit(solution)/shard_map/ppermute | solution.py:287
  261.0 32.4 %collective-permute-start.25 = (bf16[4,192,512]{2,1,0:T(8,128)(2,1)}, bf16[4,192,512]{2,1,0:T(8,128)(2,1)}, u32[]{:S(2)}, u32[]{:S(2)}) collective-permute-start(bf16[4,192,512]{2,1,0:T(8,128)(2,1)} %collective-permute-done.22.refs_1_), channel_id=1, source_target_pairs={{0,8},{4,12},{8,0},{12,4},{16,24},{20,28},{24,16},{28,20},{1,9},{5... | collective-permute-start | bytes 2359304 | tf_op jit(solution)/shard_map/ppermute | solution.py:287
  262.3 35.7 %collective-permute-start.28 = (f32[2,192,512]{2,1,0:T(8,128)}, f32[2,192,512]{2,1,0:T(8,128)S(1)}, u32[]{:S(2)}, u32[]{:S(2)}) collective-permute-start(f32[2,192,512]{2,1,0:T(8,128)} %slice.27), channel_id=1, source_target_pairs={{0,16},{4,20},{8,24},{12,28},{16,0},{20,4},{24,8},{28,12},{1,17},{... | collective-permute-start | bytes 2359304 | tf_op jit(solution)/shard_map/ppermute | solution.py:292
  276.4 21.6 %copy-start.4 = (f32[4,192,512]{2,1,0:T(8,128)S(1)}, f32[4,192,512]{2,1,0:T(8,128)}, u32[]{:S(2)}) copy-start(f32[4,192,512]{2,1,0:T(8,128)} %products.7) | copy-start | bytes 4718596
  304.6 3.7 collective-permute-start.29
  308.2 3.7 collective-permute-start.30
  308.7 20.7 %collective-permute-start.32 = (bf16[4,192,512]{2,1,0:T(8,128)(2,1)}, bf16[4,192,512]{2,1,0:T(8,128)(2,1)S(1)}, u32[]{:S(2)}, u32[]{:S(2)}) collective-permute-start(bf16[4,192,512]{2,1,0:T(8,128)(2,1)} %collective-permute-done.25.refs_1_), channel_id=1, source_target_pairs={{0,4},{4,0},{8,12},{12,8},{16,20},{20,16},{24,28},{28,24},{1,5},{5... | collective-permute-start | bytes 2359304 | tf_op jit(solution)/shard_map/ppermute | solution.py:287
  315.2 8.0 %copy-start.13 = (bf16[4,192,512]{2,1,0:T(8,128)(2,1)}, bf16[4,192,512]{2,1,0:T(8,128)(2,1)S(1)}, u32[]{:S(2)}) copy-start(bf16[4,192,512]{2,1,0:T(8,128)(2,1)S(1)} %fusion.6.refs_0_) | copy-start | bytes 2359300
  315.2 28.5 %collective-permute-start.34 = (bf16[4,192,512]{2,1,0:T(8,128)(2,1)S(1)}, bf16[4,192,512]{2,1,0:T(8,128)(2,1)S(1)}, u32[]{:S(2)}, u32[]{:S(2)}) collective-permute-start(bf16[4,192,512]{2,1,0:T(8,128)(2,1)S(1)} %fusion.6.refs_0_), channel_id=1, source_target_pairs={{0,4},{4,0},{8,12},{12,8},{16,20},{20,16},{24,28},{28,24},{1,5},{5... | collective-permute-start | bytes 2359304 | tf_op jit(solution)/shard_map/ppermute | solution.py:287
  315.7 28.0 %collective-permute-start.33 = (bf16[4,192,512]{2,1,0:T(8,128)(2,1)S(1)}, bf16[4,192,512]{2,1,0:T(8,128)(2,1)S(1)}, u32[]{:S(2)}, u32[]{:S(2)}) collective-permute-start(bf16[4,192,512]{2,1,0:T(8,128)(2,1)S(1)} %fusion.6.refs_0_), channel_id=1, source_target_pairs={{0,8},{4,12},{8,0},{12,4},{16,24},{20,28},{24,16},{28,20},{1,9},{5... | collective-permute-start | bytes 2359304 | tf_op jit(solution)/shard_map/ppermute | solution.py:287
  323.2 37.1 %collective-permute-start.31 = (bf16[4,192,512]{2,1,0:T(8,128)(2,1)S(1)}, bf16[4,192,512]{2,1,0:T(8,128)(2,1)S(1)}, u32[]{:S(2)}, u32[]{:S(2)}) collective-permute-start(bf16[4,192,512]{2,1,0:T(8,128)(2,1)S(1)} %fusion.6.refs_0_), channel_id=1, source_target_pairs={{0,16},{4,20},{8,24},{12,28},{16,0},{20,4},{24,8},{28,12},{1,17},{... | collective-permute-start | bytes 2359304 | tf_op jit(solution)/shard_map/ppermute | solution.py:292
  329.4 23.4 %copy-start.21 = (bf16[4,192,512]{2,1,0:T(8,128)(2,1)}, bf16[4,192,512]{2,1,0:T(8,128)(2,1)S(1)}, u32[]{:S(2)}) copy-start(bf16[4,192,512]{2,1,0:T(8,128)(2,1)S(1)} %collective-permute-done.32.refs_1_) | copy-start | bytes 2359300
  343.7 9.1 %copy-start.17 = (bf16[4,192,512]{2,1,0:T(8,128)(2,1)}, bf16[4,192,512]{2,1,0:T(8,128)(2,1)S(1)}, u32[]{:S(2)}) copy-start(bf16[4,192,512]{2,1,0:T(8,128)(2,1)S(1)} %collective-permute-done.34.refs_0_) | copy-start | bytes 2359300
  343.7 9.1 %copy-start.18 = (bf16[4,192,512]{2,1,0:T(8,128)(2,1)}, bf16[4,192,512]{2,1,0:T(8,128)(2,1)S(1)}, u32[]{:S(2)}) copy-start(bf16[4,192,512]{2,1,0:T(8,128)(2,1)S(1)} %collective-permute-done.33.refs_0_) | copy-start | bytes 2359300
  343.7 17.5 %collective-permute-start.35 = (bf16[4,192,512]{2,1,0:T(8,128)(2,1)S(1)}, bf16[4,192,512]{2,1,0:T(8,128)(2,1)S(1)}, u32[]{:S(2)}, u32[]{:S(2)}) collective-permute-start(bf16[4,192,512]{2,1,0:T(8,128)(2,1)S(1)} %collective-permute-done.33.refs_0_), channel_id=1, source_target_pairs={{0,4},{4,0},{8,12},{12,8},{16,20},{20,16},{24,28},{28,24},{1,5},{5... | collective-permute-start | bytes 2359304 | tf_op jit(solution)/shard_map/ppermute | solution.py:287
  360.3 3.0 copy-start.20
  361.2 9.5 %copy-start.19 = (bf16[4,192,512]{2,1,0:T(8,128)(2,1)}, bf16[4,192,512]{2,1,0:T(8,128)(2,1)S(1)}, u32[]{:S(2)}) copy-start(bf16[4,192,512]{2,1,0:T(8,128)(2,1)S(1)} %collective-permute-done.35.refs_0_) | copy-start | bytes 2359300
  361.2 16.4 %collective-permute-start.36 = (bf16[4,192,512]{2,1,0:T(8,128)(2,1)S(1)}, bf16[4,192,512]{2,1,0:T(8,128)(2,1)S(1)}, u32[]{:S(2)}, u32[]{:S(2)}) collective-permute-start(bf16[4,192,512]{2,1,0:T(8,128)(2,1)S(1)} %collective-permute-done.31.refs_1_), channel_id=1, source_target_pairs={{0,4},{4,0},{8,12},{12,8},{16,20},{20,16},{24,28},{28,24},{1,5},{5... | collective-permute-start | bytes 2359304 | tf_op jit(solution)/shard_map/ppermute | solution.py:287
  363.0 16.9 %collective-permute-start.38 = (bf16[4,192,512]{2,1,0:T(8,128)(2,1)S(1)}, bf16[4,192,512]{2,1,0:T(8,128)(2,1)S(1)}, u32[]{:S(2)}, u32[]{:S(2)}) collective-permute-start(bf16[4,192,512]{2,1,0:T(8,128)(2,1)S(1)} %collective-permute-done.31.refs_1_), channel_id=1, source_target_pairs={{0,8},{4,12},{8,0},{12,4},{16,24},{20,28},{24,16},{28,20},{1,9},{5... | collective-permute-start | bytes 2359304 | tf_op jit(solution)/shard_map/ppermute | solution.py:287
  377.6 10.6 %copy-start.22 = (bf16[4,192,512]{2,1,0:T(8,128)(2,1)}, bf16[4,192,512]{2,1,0:T(8,128)(2,1)S(1)}, u32[]{:S(2)}) copy-start(bf16[4,192,512]{2,1,0:T(8,128)(2,1)S(1)} %collective-permute-done.36.refs_1_) | copy-start | bytes 2359300
  377.6 18.1 %collective-permute-start.37 = (bf16[4,192,512]{2,1,0:T(8,128)(2,1)S(1)}, bf16[4,192,512]{2,1,0:T(8,128)(2,1)S(1)}, u32[]{:S(2)}, u32[]{:S(2)}) collective-permute-start(bf16[4,192,512]{2,1,0:T(8,128)(2,1)S(1)} %collective-permute-done.36.refs_1_), channel_id=1, source_target_pairs={{0,8},{4,12},{8,0},{12,4},{16,24},{20,28},{24,16},{28,20},{1,9},{5... | collective-permute-start | bytes 2359304 | tf_op jit(solution)/shard_map/ppermute | solution.py:287
  396.6 7.6 %copy-start.1 = (bf16[192,2112]{1,0:T(8,128)(2,1)S(1)}, bf16[192,2112]{1,0:T(8,128)(2,1)}, u32[]{:S(2)}) copy-start(bf16[192,2112]{1,0:T(8,128)(2,1)} %param.11) | copy-start | bytes 2433028
  (4 other events, 3.6 us)
